TPU v7x, 32 devices: a whole 2x2x4 slice. The times are simulated.
32 devices in a mesh: gx: 16 (over z, y, core), gy: 2 (over x).
Axes of the slice: x: 2, y: 2, z: 4, core: 2. Of those that a mesh axis runs over, the one named last changes fastest.
Arguments:
- e_field: float32 [3, 64, 128, 256], P(None, None, 'gx', 'gy'), may hold values from -6 to 6
- h_field: float32 [3, 64, 128, 256], P(None, None, 'gx', 'gy'), may hold values from -6 to 6
- material: int32 [64, 128, 256], P(None, 'gx', 'gy'), may hold values from 0 to 7
- permittivity: float32 [8], replicated, may hold values from 1 to 12
- conductivity: float32 [8], replicated, may hold values from 0.05 to 2
- src_shift: int32 [256, 2], P(('gx', 'gy')), may hold values from 0 to 128
- src_weight: float32 [256], P(('gx', 'gy')), may hold values from 0.05 to 5
- pupil_mask: int32 [128, 128], replicated, may hold values 0 or 1
Outputs:
- image: float32 [512, 512], P(('gx', 'gy'))
- e_final: float32 [3, 64, 128, 256], P(None, None, 'gx', 'gy')
- h_final: float32 [3, 64, 128, 256], P(None, None, 'gx', 'gy')
All inputs are finite; a program needn't handle non-finite values.
Results may differ from a plain program's by a relative error of at most 0.0019.
Values may be sent and summed in bfloat16 or wider, within the bound.
A program may use at most 128 MiB of HBM per device.

v0:
```python
import math

import jax
import jax.numpy as jnp
from jax import lax
from jax.sharding import PartitionSpec as P

STEPS = 4
K = 256
PW = 128
IMG = 512


COURANT = 0.5


def passed_along(value, axis, steps):
    count = lax.axis_size(axis)
    first, last = (max(0, -steps), min(count, count - steps))
    return lax.ppermute(value, axis, [(source, source + steps) for source in range(first, last)])


def coefficients(material, permittivity, conductivity):
    loss = conductivity / (2.0 * permittivity)
    keep_tab = (1.0 - loss) / (1.0 + loss)
    drive_tab = COURANT / (permittivity * (1.0 + loss))
    keep = jnp.zeros(material.shape, jnp.float32)
    drive = jnp.zeros(material.shape, jnp.float32)
    for index in range(permittivity.shape[0]):
        chosen = material == index
        keep = jnp.where(chosen, keep_tab[index], keep)
        drive = jnp.where(chosen, drive_tab[index], drive)
    return (keep, drive)


def zero_face(field, axis):
    shape = list(field.shape)
    shape[axis] = 1
    return jnp.zeros(shape, field.dtype)


def ahead(field, face, axis):
    count = field.shape[axis]
    return jnp.concatenate((lax.slice_in_dim(field, 1, count, axis=axis), face), axis=axis)


def behind(field, face, axis):
    count = field.shape[axis]
    return jnp.concatenate((face, lax.slice_in_dim(field, 0, count - 1, axis=axis)), axis=axis)


def magnetic(e, h, faces_x, faces_y):
    ex, ey, ez = (e[0], e[1], e[2])
    ey_x = ahead(ey, faces_x[0], 1)
    ez_x = ahead(ez, faces_x[1], 1)
    ex_y = ahead(ex, faces_y[0], 2)
    ez_y = ahead(ez, faces_y[1], 2)
    ex_z = ahead(ex, zero_face(ex, 0), 0)
    ey_z = ahead(ey, zero_face(ey, 0), 0)
    new_x = h[0] - COURANT * (ez_y - ez - (ey_z - ey))
    new_y = h[1] - COURANT * (ex_z - ex - (ez_x - ez))
    new_z = h[2] - COURANT * (ey_x - ey - (ex_y - ex))
    return jnp.stack((new_x, new_y, new_z))


def electric(e, h, keep, drive, faces_x, faces_y):
    hx, hy, hz = (h[0], h[1], h[2])
    hy_x = behind(hy, faces_x[0], 1)
    hz_x = behind(hz, faces_x[1], 1)
    hx_y = behind(hx, faces_y[0], 2)
    hz_y = behind(hz, faces_y[1], 2)
    hx_z = behind(hx, zero_face(hx, 0), 0)
    hy_z = behind(hy, zero_face(hy, 0), 0)
    new_x = keep * e[0] + drive * (hz - hz_y - (hy - hy_z))
    new_y = keep * e[1] + drive * (hx - hx_z - (hz - hz_x))
    new_z = keep * e[2] + drive * (hy - hy_x - (hx - hx_y))
    return jnp.stack((new_x, new_y, new_z))


def exit_spectrum(near, row_start, col_start, rows_all, cols_all, order):
    count_x = near.shape[1]
    count_y = near.shape[2]
    freqs = jnp.arange(order, dtype=jnp.int32) - order // 2
    cols = col_start + jnp.arange(count_y, dtype=jnp.int32)
    phase_y = jnp.mod(cols[:, None] * freqs[None, :], cols_all).astype(jnp.float32) * (
        2.0 * math.pi / cols_all
    )
    table_y = jnp.concatenate((jnp.cos(phase_y), -jnp.sin(phase_y)), axis=1)
    half = jnp.dot(near.reshape(2 * count_x, count_y), table_y, precision=lax.Precision.HIGHEST)
    half = half.reshape(2, count_x, 2 * order)
    rows = row_start + jnp.arange(count_x, dtype=jnp.int32)
    phase_x = jnp.mod(freqs[:, None] * rows[None, :], rows_all).astype(jnp.float32) * (
        2.0 * math.pi / rows_all
    )
    table_x = jnp.concatenate((jnp.cos(phase_x), jnp.sin(phase_x)), axis=0)
    blocks = jnp.einsum("ax,pxb->pab", table_x, half, precision=lax.Precision.HIGHEST)
    real = blocks[:, :order, :order] + blocks[:, order:, order:]
    imag = blocks[:, :order, order:] - blocks[:, order:, :order]
    stacked = jnp.stack((real[0], imag[0], real[1], imag[1]), axis=1)
    return stacked * (1.0 / math.sqrt(rows_all * cols_all))


def pupil_tables(window, pixels):
    offsets = jnp.arange(window, dtype=jnp.int32) - window // 2
    places = jnp.arange(pixels, dtype=jnp.int32)
    phase = jnp.mod(offsets[:, None] * places[None, :], pixels).astype(jnp.float32) * (
        2.0 * math.pi / pixels
    )
    cosine = jnp.cos(phase)
    sine = jnp.sin(phase)
    second = jnp.concatenate(
        (jnp.concatenate((cosine, sine), axis=1), jnp.concatenate((-sine, cosine), axis=1)), axis=0
    )
    row_cos = cosine.T / window
    row_sin = sine.T / window
    real_row = jnp.stack((row_cos, -row_sin), axis=2)
    imag_row = jnp.stack((row_sin, row_cos), axis=2)
    first = jnp.stack((real_row, imag_row)).reshape(2, pixels, 2 * window)
    return (second.astype(jnp.bfloat16), first.astype(jnp.bfloat16))


def pupil_halves(spectrum_b, shifts, pupil_mask, second, window, pixels):
    zero = jnp.zeros((), jnp.int32)

    def cut(shift):
        return lax.dynamic_slice(spectrum_b, (shift[0], zero, shift[1]), (window, 4, window))

    pieces = jax.vmap(cut)(shifts)
    pieces = pieces * pupil_mask.astype(jnp.bfloat16)[None, :, None, :]
    count = shifts.shape[0]
    arranged = (
        pieces.reshape(count, window, 2, 2, window)
        .transpose(0, 2, 1, 3, 4)
        .reshape(count * 2 * window, 2 * window)
    )
    halves = jnp.dot(arranged, second, preferred_element_type=jnp.float32).astype(jnp.bfloat16)
    return halves.reshape(count * 2, 2 * window, pixels)


def local(
    e_field, h_field, material, permittivity, conductivity, src_shift, src_weight, pupil_mask
):
    tile_x = e_field.shape[2]
    tile_y = e_field.shape[3]
    depth = e_field.shape[1]
    rows_all = tile_x * lax.axis_size("gx")
    cols_all = tile_y * lax.axis_size("gy")
    devices = lax.axis_size("gx") * lax.axis_size("gy")
    keep, drive = coefficients(material, permittivity, conductivity)
    e = e_field
    h = h_field
    for step in range(STEPS):
        upper = passed_along(jnp.stack((e[1][:, :1], e[2][:, :1])), "gx", -1)
        right = passed_along(jnp.stack((e[0][:, :, :1], e[2][:, :, :1])), "gy", -1)
        h = magnetic(e, h, (upper[0], upper[1]), (right[0], right[1]))
        lower = passed_along(jnp.stack((h[1][:, -1:], h[2][:, -1:])), "gx", 1)
        left = passed_along(jnp.stack((h[0][:, :, -1:], h[2][:, :, -1:])), "gy", 1)
        e = electric(e, h, keep, drive, (lower[0], lower[1]), (left[0], left[1]))
    near = e[0:2, depth - 1]
    partial_value = exit_spectrum(
        near, lax.axis_index("gx") * tile_x, lax.axis_index("gy") * tile_y, rows_all, cols_all, K
    )
    spectrum_b = lax.psum(partial_value, ("gx", "gy")).astype(jnp.bfloat16)
    second, first = pupil_tables(PW, IMG)
    halves = pupil_halves(spectrum_b, src_shift, pupil_mask, second, PW, IMG)
    total_sources = src_shift.shape[0] * devices
    factors = jnp.repeat(src_weight / total_sources, 2)
    count = IMG // devices * lax.axis_size(("gx", "gy"))
    rows = first.reshape(2 * count, 2 * PW)

    def add(total, item):
        field = jnp.dot(rows, item[0], preferred_element_type=jnp.float32)
        return (
            total + item[1] * (field[:count] * field[:count] + field[count:] * field[count:]),
            None,
        )

    total, _ = lax.scan(add, jnp.zeros((count, IMG), jnp.float32), (halves, factors))
    image = lax.psum_scatter(total, ("gx", "gy"), scatter_dimension=0, tiled=True)
    return (image, e, h)


def solution(mesh):
    return jax.shard_map(
        local,
        mesh=mesh,
        in_specs=(
            P(None, None, "gx", "gy"),
            P(None, None, "gx", "gy"),
            P(None, "gx", "gy"),
            P(),
            P(),
            P(("gx", "gy"), None),
            P(("gx", "gy")),
            P(),
        ),
        out_specs=(P(("gx", "gy"), None), P(None, None, "gx", "gy"), P(None, None, "gx", "gy")),
        check_vma=False,
    )
```

profile of v0, /device:TPU:0, one launch (start us, length us, event | category | flops | bytes accessed | tf_op | source)
XLA Modules:
  0.0 444.7 jit_solution(12155305380205002507)
XLA Ops:
  16.0 2.0 fusion.124
  23.1 7.1 %select_select_fusion = (f32[64,8,128]{2,1,0:T(8,128)S(1)}, pred[64,8,128]{2,1,0:T(8,128)(4,1)}, pred[64,8,128]{2,1,0:T(8,128)(4,1)}, pred[64,8,128]{2,1,0:T(8,1...) fusion(f32[]{:T(128)} %bitcast.16, f32[]{:T(128)} %bitcast.15, ...), kind=kLoop, calls=%fused_computation.184 | loop fusion | flops 1048576 | bytes 1048608 | tf_op jit(solution)/shard_map/jit(_where)/select_n | solution.py:32
  38.2 2.1 fusion.26
  40.9 5.4 %collective-permute-start.2 = (f32[2,64,8,1]{1,2,3,0:T(8,128)S(1)}, f32[2,64,8,1]{1,2,3,0:T(8,128)S(1)}, u32[]{:S(2)}, u32[]{:S(2)}) collective-permute-start(f32[2,64,8,1]{1,2,3,0:T(8,128)S(1)} %pad_maximum_fusion.15), channel_id=1, source_target_pairs={{0,1},{2,3},{4,5},{6,7},{8,9},{10,11},{12,13},{14,15},{16,17},{18,... | collective-permute-start | bytes 12296 | tf_op jit(solution)/shard_map/ppermute | solution.py:20
  47.8 2.7 collective-permute-start.3
  50.9 6.3 %fusion.92 = (f32[64,8,128]{2,1,0:T(8,128)S(1)}, f32[64,8,128]{2,1,0:T(8,128)S(1)}) fusion(f32[64,8,128]{2,0,1:T(8,128)S(1)} %fusion.28, f32[3,64,8,128]{3,2,1,0:T(8,128)} %param.10, pred[64,8,128]{2,1,0:T(8,128)(4,1)} %get-tuple-element.141, pred[64,8,128]{2,1,0:T(8,128)(4,1)} %get-tuple-element.140, pred[64,8,128]{2,1,0:T(8,128)(4,1)} %get-tuple-element.139, ...), kind=kLoop, calls=%fused_computation.160 | loop fusion | flops 655360 | bytes 1572896 | tf_op jit(solution)/shard_map/add | solution.py:74
  59.9 2.4 copy_multiply_fusion.2
  69.8 2.1 collective-permute-done.4
  74.3 4.3 collective-permute-start.6
  81.4 4.5 %collective-permute-start.7 = (f32[2,64,1,128]{3,1,2,0:T(8,128)S(1)}, f32[2,64,1,128]{3,1,2,0:T(8,128)S(1)}, u32[]{:S(2)}, u32[]{:S(2)}) collective-permute-start(f32[2,64,1,128]{3,1,2,0:T(8,128)S(1)} %pad_maximum_fusion.8), channel_id=1, source_target_pairs={{0,2},{2,4},{4,6},{6,8},{8,10},{10,12},{12,14},{14,16},{16,18},{18... | collective-permute-start | bytes 196616 | tf_op jit(solution)/shard_map/ppermute | solution.py:20
  87.7 2.5 copy_multiply_fusion.1
  111.6 4.6 %collective-permute-start.10 = (f32[2,64,8,1]{1,2,3,0:T(8,128)S(1)}, f32[2,64,8,1]{1,2,3,0:T(8,128)S(1)}, u32[]{:S(2)}, u32[]{:S(2)}) collective-permute-start(f32[2,64,8,1]{1,2,3,0:T(8,128)S(1)} %pad_maximum_fusion.19), channel_id=1, source_target_pairs={{0,1},{2,3},{4,5},{6,7},{8,9},{10,11},{12,13},{14,15},{16,17},{18,... | collective-permute-start | bytes 12296 | tf_op jit(solution)/shard_map/ppermute | solution.py:20
  117.6 4.6 %collective-permute-start.11 = (f32[2,64,1,128]{3,1,2,0:T(8,128)S(1)}, f32[2,64,1,128]{3,1,2,0:T(8,128)S(1)}, u32[]{:S(2)}, u32[]{:S(2)}) collective-permute-start(f32[2,64,1,128]{3,1,2,0:T(8,128)S(1)} %pad_maximum_fusion.10), channel_id=1, source_target_pairs={{0,2},{2,4},{4,6},{6,8},{8,10},{10,12},{12,14},{14,16},{16,18},{18... | collective-permute-start | bytes 196616 | tf_op jit(solution)/shard_map/ppermute | solution.py:20
  136.1 2.0 fusion.73
  139.4 4.3 collective-permute-start.14
  146.0 5.0 %collective-permute-start.15 = (f32[2,64,1,128]{3,1,2,0:T(8,128)S(1)}, f32[2,64,1,128]{3,1,2,0:T(8,128)S(1)}, u32[]{:S(2)}, u32[]{:S(2)}) collective-permute-start(f32[2,64,1,128]{3,1,2,0:T(8,128)S(1)} %pad_maximum_fusion.12), channel_id=1, source_target_pairs={{0,2},{2,4},{4,6},{6,8},{8,10},{10,12},{12,14},{14,16},{16,18},{18... | collective-permute-start | bytes 196616 | tf_op jit(solution)/shard_map/ppermute | solution.py:20
  152.8 2.4 fusion.91
  157.7 54.5 %all-reduce.17 = bf16[256,4,256]{0,2,1:T(8,128)(2,1)S(1)} all-reduce(f32[256,4,256]{0,2,1:T(8,128)S(1)} %maximum_multiply_fusion), channel_id=1, replica_groups=mesh['gx'=16,'gy'=2] {'gx','gy'}, use_global_device_ids=true, to_apply=%region_0.1 | all-reduce | flops 262144 | bytes 1572864 | tf_op jit(solution)/shard_map/psum | solution.py:163
  212.2 22.4 %while.12 = (s32[]{:T(128)}, bf16[256,4,256]{0,2,1:T(8,128)(2,1)S(1)}, s32[8,3]{0,1:T(4,128)S(1)}, bf16[8,128,4,128]{3,2,1,0:T(4,128)(2,1)}, s32[]{:T(128)}) while((s32[]{:T(128)}, bf16[256,4,256]{0,2,1:T(8,128)(2,1)S(1)}, s32[8,3]{0,1:T(4,128)S(1)}, bf16[8,128,4,128]{3,2,1,0:T(4,128)(2,1)}, s32[]{:T(128)}) %tuple.128), condition=%wide.while_cond, body=%wide.while_body.sunk | while | flops 2 | bytes 787057 | solution.py:126
  234.7 2.1 copy_multiply_fusion
  236.8 3.3 convolution_convert_fusion
  240.1 7.1 %reshape.181 = bf16[16,256,512]{2,1,0:T(8,128)(2,1)} reshape(bf16[2048,1024]{1,0:T(8,128)(2,1)} %convolution_convert_fusion) | data formatting | bytes 8388608 | tf_op jit(solution)/shard_map/reshape | solution.py:137
  247.2 55.5 %while.13 = (s32[]{:T(128)}, f32[512,512]{0,1:T(8,128)S(1)}, f32[16]{0:T(128)S(1)}, bf16[16,256,512]{2,1,0:T(8,128)(2,1)}, bf16[1024,256]{1,0:T(8,128)(2,1)}, /*index=5*/s32[]{:T(128)}, s32[]{:T(128)}) while((s32[]{:T(128)}, f32[512,512]{0,1:T(8,128)S(1)}, f32[16]{0:T(128)S(1)}, bf16[16,256,512]{2,1,0:T(8,128)(2,1)}, ...), condition=%wide.region_2.3_spmd.clone, body=%wide.region_1.2_spmd.clone.sunk | while | flops 270008320 | bytes 7078503 | solution.py:178
  307.0 130.9 %reduce-scatter.2.cloned.1.call-done = f32[16,512]{1,0:T(8,128)} async-done(((f32[512,512]{1,0:T(8,128)}), f32[16,512]{1,0:T(8,128)}) %reduce-scatter.2.cloned.1.call-update) | async-done | bytes 32784 | tf_op jit(solution)/shard_map/reduce_scatter | solution.py:179
  (335 shorter events, 166.9 us)
Async XLA Ops:
  7.2 430.7 %reduce-scatter.2.cloned.1.call-start = ((), (), s32[]{:S(2)}) async-start(), calls=%async_computation.1 | async-start | bytes 1081344 | tf_op jit(solution)/shard_map/reduce_scatter | solution.py:179
  8.5 29.8 %copy-start.7 = (f32[1,64,8,128]{3,2,1,0:T(8,128)}, f32[1,64,8,128]{3,2,1,0:T(8,128)S(1)}, u32[]{:S(2)}) copy-start(f32[1,64,8,128]{3,2,1,0:T(8,128)S(1)} %get-tuple-element.160) | copy-start | bytes 786436
  9.3 28.1 %collective-permute-start = (f32[2,64,1,128]{3,1,2,0:T(8,128)}, f32[2,64,1,128]{3,1,2,0:T(8,128)}, u32[]{:S(2)}, u32[]{:S(2)}) collective-permute-start(f32[2,64,1,128]{3,1,2,0:T(8,128)} %pad_maximum_fusion.5), channel_id=1, source_target_pairs={{2,0},{4,2},{6,4},{8,6},{10,8},{12,10},{14,12},{16,14},{18,16},{20... | collective-permute-start | bytes 196616 | tf_op jit(solution)/shard_map/ppermute | solution.py:20
  11.6 24.1 %collective-permute-start.1 = (f32[2,64,8,1]{1,2,3,0:T(8,128)}, f32[2,64,8,1]{1,2,3,0:T(8,128)}, u32[]{:S(2)}, u32[]{:S(2)}) collective-permute-start(f32[2,64,8,1]{1,2,3,0:T(8,128)} %pad_maximum_fusion.14), channel_id=1, source_target_pairs={{1,0},{3,2},{5,4},{7,6},{9,8},{11,10},{13,12},{15,14},{17,16},{19,... | collective-permute-start | bytes 12296 | tf_op jit(solution)/shard_map/ppermute | solution.py:20
  40.9 9.7 %collective-permute-start.2 = (f32[2,64,8,1]{1,2,3,0:T(8,128)S(1)}, f32[2,64,8,1]{1,2,3,0:T(8,128)S(1)}, u32[]{:S(2)}, u32[]{:S(2)}) collective-permute-start(f32[2,64,8,1]{1,2,3,0:T(8,128)S(1)} %pad_maximum_fusion.15), channel_id=1, source_target_pairs={{0,1},{2,3},{4,5},{6,7},{8,9},{10,11},{12,13},{14,15},{16,17},{18,... | collective-permute-start | bytes 12296 | tf_op jit(solution)/shard_map/ppermute | solution.py:20
  47.8 12.1 %collective-permute-start.3 = (f32[2,64,1,128]{3,1,2,0:T(8,128)S(1)}, f32[2,64,1,128]{3,1,2,0:T(8,128)S(1)}, u32[]{:S(2)}, u32[]{:S(2)}) collective-permute-start(f32[2,64,1,128]{3,1,2,0:T(8,128)S(1)} %pad_maximum_fusion.6), channel_id=1, source_target_pairs={{0,2},{2,4},{4,6},{6,8},{8,10},{10,12},{12,14},{14,16},{16,18},{18... | collective-permute-start | bytes 196616 | tf_op jit(solution)/shard_map/ppermute | solution.py:20
  62.4 5.6 %collective-permute-start.5 = (f32[2,64,8,1]{1,2,3,0:T(8,128)S(1)}, f32[2,64,8,1]{1,2,3,0:T(8,128)S(1)}, u32[]{:S(2)}, u32[]{:S(2)}) collective-permute-start(f32[2,64,8,1]{1,2,3,0:T(8,128)S(1)} %pad_maximum_fusion.16), channel_id=1, source_target_pairs={{1,0},{3,2},{5,4},{7,6},{9,8},{11,10},{13,12},{15,14},{17,16},{19,... | collective-permute-start | bytes 12296 | tf_op jit(solution)/shard_map/ppermute | solution.py:20
  66.7 5.2 %collective-permute-start.4 = (f32[2,64,1,128]{3,1,2,0:T(8,128)S(1)}, f32[2,64,1,128]{3,1,2,0:T(8,128)S(1)}, u32[]{:S(2)}, u32[]{:S(2)}) collective-permute-start(f32[2,64,1,128]{3,1,2,0:T(8,128)S(1)} %pad_maximum_fusion.7), channel_id=1, source_target_pairs={{2,0},{4,2},{6,4},{8,6},{10,8},{12,10},{14,12},{16,14},{18,16},{20... | collective-permute-start | bytes 196616 | tf_op jit(solution)/shard_map/ppermute | solution.py:20
  74.3 11.6 %collective-permute-start.6 = (f32[2,64,8,1]{1,2,3,0:T(8,128)S(1)}, f32[2,64,8,1]{1,2,3,0:T(8,128)S(1)}, u32[]{:S(2)}, u32[]{:S(2)}) collective-permute-start(f32[2,64,8,1]{1,2,3,0:T(8,128)S(1)} %pad_maximum_fusion.17), channel_id=1, source_target_pairs={{0,1},{2,3},{4,5},{6,7},{8,9},{10,11},{12,13},{14,15},{16,17},{18,... | collective-permute-start | bytes 12296 | tf_op jit(solution)/shard_map/ppermute | solution.py:20
  81.4 6.3 %collective-permute-start.7 = (f32[2,64,1,128]{3,1,2,0:T(8,128)S(1)}, f32[2,64,1,128]{3,1,2,0:T(8,128)S(1)}, u32[]{:S(2)}, u32[]{:S(2)}) collective-permute-start(f32[2,64,1,128]{3,1,2,0:T(8,128)S(1)} %pad_maximum_fusion.8), channel_id=1, source_target_pairs={{0,2},{2,4},{4,6},{6,8},{8,10},{10,12},{12,14},{14,16},{16,18},{18... | collective-permute-start | bytes 196616 | tf_op jit(solution)/shard_map/ppermute | solution.py:20
  91.5 16.6 %copy-start.6 = (f32[64,8,128]{2,1,0:T(8,128)S(1)}, f32[64,8,128]{2,1,0:T(8,128)}, u32[]{:S(2)}) copy-start(f32[64,8,128]{2,1,0:T(8,128)} %copy-done.5) | copy-start | bytes 786436
  93.2 9.0 %collective-permute-start.9 = (f32[2,64,8,1]{1,2,3,0:T(8,128)S(1)}, f32[2,64,8,1]{1,2,3,0:T(8,128)S(1)}, u32[]{:S(2)}, u32[]{:S(2)}) collective-permute-start(f32[2,64,8,1]{1,2,3,0:T(8,128)S(1)} %pad_maximum_fusion.18), channel_id=1, source_target_pairs={{1,0},{3,2},{5,4},{7,6},{9,8},{11,10},{13,12},{15,14},{17,16},{19,... | collective-permute-start | bytes 12296 | tf_op jit(solution)/shard_map/ppermute | solution.py:20
  100.8 4.5 %collective-permute-start.8 = (f32[2,64,1,128]{3,1,2,0:T(8,128)}, f32[2,64,1,128]{3,1,2,0:T(8,128)}, u32[]{:S(2)}, u32[]{:S(2)}) collective-permute-start(f32[2,64,1,128]{3,1,2,0:T(8,128)} %pad_maximum_fusion.9), channel_id=1, source_target_pairs={{2,0},{4,2},{6,4},{8,6},{10,8},{12,10},{14,12},{16,14},{18,16},{20... | collective-permute-start | bytes 196616 | tf_op jit(solution)/shard_map/ppermute | solution.py:20
  109.7 14.3 %copy-start.3 = (f32[64,8,128]{2,1,0:T(8,128)}, f32[64,8,128]{2,1,0:T(8,128)S(1)}, u32[]{:S(2)}) copy-start(f32[64,8,128]{2,1,0:T(8,128)S(1)} %get-tuple-element.172) | copy-start | bytes 786436
  111.6 10.7 %collective-permute-start.10 = (f32[2,64,8,1]{1,2,3,0:T(8,128)S(1)}, f32[2,64,8,1]{1,2,3,0:T(8,128)S(1)}, u32[]{:S(2)}, u32[]{:S(2)}) collective-permute-start(f32[2,64,8,1]{1,2,3,0:T(8,128)S(1)} %pad_maximum_fusion.19), channel_id=1, source_target_pairs={{0,1},{2,3},{4,5},{6,7},{8,9},{10,11},{12,13},{14,15},{16,17},{18,... | collective-permute-start | bytes 12296 | tf_op jit(solution)/shard_map/ppermute | solution.py:20
  117.6 6.4 %collective-permute-start.11 = (f32[2,64,1,128]{3,1,2,0:T(8,128)S(1)}, f32[2,64,1,128]{3,1,2,0:T(8,128)S(1)}, u32[]{:S(2)}, u32[]{:S(2)}) collective-permute-start(f32[2,64,1,128]{3,1,2,0:T(8,128)S(1)} %pad_maximum_fusion.10), channel_id=1, source_target_pairs={{0,2},{2,4},{4,6},{6,8},{8,10},{10,12},{12,14},{14,16},{16,18},{18... | collective-permute-start | bytes 196616 | tf_op jit(solution)/shard_map/ppermute | solution.py:20
  126.3 7.2 %collective-permute-start.13 = (f32[2,64,8,1]{1,2,3,0:T(8,128)S(1)}, f32[2,64,8,1]{1,2,3,0:T(8,128)S(1)}, u32[]{:S(2)}, u32[]{:S(2)}) collective-permute-start(f32[2,64,8,1]{1,2,3,0:T(8,128)S(1)} %pad_maximum_fusion.20), channel_id=1, source_target_pairs={{1,0},{3,2},{5,4},{7,6},{9,8},{11,10},{13,12},{15,14},{17,16},{19,... | collective-permute-start | bytes 12296 | tf_op jit(solution)/shard_map/ppermute | solution.py:20
  132.2 3.9 collective-permute-start.12
  138.2 17.0 %copy-start.1 = (f32[64,8,128]{2,1,0:T(8,128)}, f32[64,8,128]{2,1,0:T(8,128)S(1)}, u32[]{:S(2)}) copy-start(f32[64,8,128]{2,1,0:T(8,128)S(1)} %get-tuple-element.169) | copy-start | bytes 786436
  138.2 74.0 %copy-start = (f32[64,8,128]{2,1,0:T(8,128)}, f32[64,8,128]{2,1,0:T(8,128)S(1)}, u32[]{:S(2)}) copy-start(f32[64,8,128]{2,1,0:T(8,128)S(1)} %get-tuple-element.167) | copy-start | bytes 786436
  139.4 11.6 %collective-permute-start.14 = (f32[2,64,8,1]{1,2,3,0:T(8,128)S(1)}, f32[2,64,8,1]{1,2,3,0:T(8,128)S(1)}, u32[]{:S(2)}, u32[]{:S(2)}) collective-permute-start(f32[2,64,8,1]{1,2,3,0:T(8,128)S(1)} %pad_maximum_fusion.21), channel_id=1, source_target_pairs={{0,1},{2,3},{4,5},{6,7},{8,9},{10,11},{12,13},{14,15},{16,17},{18,... | collective-permute-start | bytes 12296 | tf_op jit(solution)/shard_map/ppermute | solution.py:20
  146.0 6.8 %collective-permute-start.15 = (f32[2,64,1,128]{3,1,2,0:T(8,128)S(1)}, f32[2,64,1,128]{3,1,2,0:T(8,128)S(1)}, u32[]{:S(2)}, u32[]{:S(2)}) collective-permute-start(f32[2,64,1,128]{3,1,2,0:T(8,128)S(1)} %pad_maximum_fusion.12), channel_id=1, source_target_pairs={{0,2},{2,4},{4,6},{6,8},{8,10},{10,12},{12,14},{14,16},{16,18},{18... | collective-permute-start | bytes 196616 | tf_op jit(solution)/shard_map/ppermute | solution.py:20
  157.7 79.1 %copy-start.17 = (bf16[128,512]{1,0:T(8,128)(2,1)S(1)}, bf16[128,512]{1,0:T(8,128)(2,1)}, u32[]{:S(2)}) copy-start(bf16[128,512]{1,0:T(8,128)(2,1)} %get-tuple-element.224) | copy-start | bytes 393220
  157.7 79.1 %copy-start.18 = (bf16[128,512]{1,0:T(8,128)(2,1)S(1)}, bf16[128,512]{1,0:T(8,128)(2,1)}, u32[]{:S(2)}) copy-start(bf16[128,512]{1,0:T(8,128)(2,1)} %get-tuple-element.225) | copy-start | bytes 393220
  (20 other events, 138.8 us)
Sparse Core Ops, SparseCore 0:
  304.2 133.5 reduce-scatter.1
where the time goes:
time: 447 us; the launch traced here: 445 us
  waiting for transfers between devices  134 us (30%)
  local copies, waits for them, and re-layouts  92 us (21%)
  other arithmetic  71.7 us (16%)
  blocking collectives  54.5 us (12%)
  starting transfers between devices  45.9 us (10%)
  matrix products  31.2 us (7%)
  between operations  15.1 us (3%)
    reduce_scatter x1, waiting for transfers between devices, local(): lax.psum_scatter(total, ('gx', 'gy'), scatter_dimension=0, tiled=True)  131 us
    psum x1, blocking collectives, local(): spectrum_b = lax.psum(partial_value, ('gx', 'gy')).astype(jnp.bfloat16)  54.5 us
    ppermute x16, starting transfers between devices, passed_along(): lax.ppermute(value, axis, [(source, source + steps) for source in range(f...  45.9 us
    dot_general x16, matrix products, add(): field = jnp.dot(rows, item[0], preferred_element_type=jnp.float32)  25.8 us
    gather x40, local copies, waits for them, and re-layouts  22.4 us
    add x16, other arithmetic, add(): total + item[1] * (field[:count] * field[:count] + field[count:] * field[...  19.9 us
    slice x24, local copies, waits for them, and re-layouts, ahead(): lax.slice_in_dim(field, 1, count, axis=axis)  16.5 us
    dynamic_slice x16, local copies, waits for them, and re-layouts, local(): lax.scan(add, jnp.zeros((count, IMG), jnp.float32), (halves, factors))  9.42 us
  transfers between devices with their start and end apart: 17, of which 3 were waited for; matrix products, arithmetic and copies ran while one was open for 16% of the time, Pallas kernels for 0%

commit v1 on v0

v1 whole, which is shorter than its diff:
```python
import math

import jax
import jax.numpy as jnp
import numpy as np
from jax import lax
from jax.sharding import PartitionSpec as P

STEPS = 4
K = 256
PW = 128
IMG = 512


COURANT = 0.5


def passed_along(value, axis, steps):
    count = lax.axis_size(axis)
    first, last = (max(0, -steps), min(count, count - steps))
    return lax.ppermute(value, axis, [(source, source + steps) for source in range(first, last)])


def coefficients(material, permittivity, conductivity):
    loss = conductivity / (2.0 * permittivity)
    keep_tab = (1.0 - loss) / (1.0 + loss)
    drive_tab = COURANT / (permittivity * (1.0 + loss))
    keep = jnp.zeros(material.shape, jnp.float32)
    drive = jnp.zeros(material.shape, jnp.float32)
    for index in range(permittivity.shape[0]):
        chosen = material == index
        keep = jnp.where(chosen, keep_tab[index], keep)
        drive = jnp.where(chosen, drive_tab[index], drive)
    return (keep, drive)


def zero_face(field, axis):
    shape = list(field.shape)
    shape[axis] = 1
    return jnp.zeros(shape, field.dtype)


def ahead(field, face, axis):
    count = field.shape[axis]
    return jnp.concatenate((lax.slice_in_dim(field, 1, count, axis=axis), face), axis=axis)


def behind(field, face, axis):
    count = field.shape[axis]
    return jnp.concatenate((face, lax.slice_in_dim(field, 0, count - 1, axis=axis)), axis=axis)


def magnetic(e, h, faces_x, faces_y):
    ex, ey, ez = (e[0], e[1], e[2])
    ey_x = ahead(ey, faces_x[0], 1)
    ez_x = ahead(ez, faces_x[1], 1)
    ex_y = ahead(ex, faces_y[0], 2)
    ez_y = ahead(ez, faces_y[1], 2)
    ex_z = ahead(ex, zero_face(ex, 0), 0)
    ey_z = ahead(ey, zero_face(ey, 0), 0)
    new_x = h[0] - COURANT * (ez_y - ez - (ey_z - ey))
    new_y = h[1] - COURANT * (ex_z - ex - (ez_x - ez))
    new_z = h[2] - COURANT * (ey_x - ey - (ex_y - ex))
    return jnp.stack((new_x, new_y, new_z))


def electric(e, h, keep, drive, faces_x, faces_y):
    hx, hy, hz = (h[0], h[1], h[2])
    hy_x = behind(hy, faces_x[0], 1)
    hz_x = behind(hz, faces_x[1], 1)
    hx_y = behind(hx, faces_y[0], 2)
    hz_y = behind(hz, faces_y[1], 2)
    hx_z = behind(hx, zero_face(hx, 0), 0)
    hy_z = behind(hy, zero_face(hy, 0), 0)
    new_x = keep * e[0] + drive * (hz - hz_y - (hy - hy_z))
    new_y = keep * e[1] + drive * (hx - hx_z - (hz - hz_x))
    new_z = keep * e[2] + drive * (hy - hy_x - (hx - hx_y))
    return jnp.stack((new_x, new_y, new_z))


def spectrum_tables(rows_all, cols_all, order):
    freqs = np.arange(order) - order // 2
    phase_y = 2.0 * np.pi * np.mod(np.arange(cols_all)[:, None] * freqs[None, :], cols_all) / cols_all
    table_y = np.concatenate((np.cos(phase_y), -np.sin(phase_y)), axis=1)
    phase_x = 2.0 * np.pi * np.mod(freqs[:, None] * np.arange(rows_all)[None, :], rows_all) / rows_all
    table_x = np.concatenate((np.cos(phase_x), np.sin(phase_x)), axis=1) / np.sqrt(rows_all * cols_all)
    return table_y.astype(np.float32), table_x.astype(np.float32)


def image_tables(window, pixels):
    coarse = pixels // 2
    offsets = np.arange(window) - window // 2
    phase = 2.0 * np.pi * np.mod(offsets[:, None] * np.arange(coarse)[None, :], coarse) / coarse
    cosine, sine = np.cos(phase), np.sin(phase)
    second = np.block([[cosine, sine], [-sine, cosine]])
    first = np.block([[cosine.T, -sine.T], [sine.T, cosine.T]]) / window
    gaps = np.arange(pixels)[:, None] - 2 * np.arange(coarse)[None, :]
    spread = np.ones(gaps.shape)
    for order in range(1, coarse // 2):
        spread += 2.0 * np.cos(2.0 * np.pi * np.mod(order * gaps, pixels) / pixels)
    spread += np.cos(np.pi * gaps / 2.0)
    spread = spread / coarse
    return second.astype(jnp.bfloat16), first.astype(jnp.bfloat16), spread.astype(np.float32)


def exit_spectrum(near, order):
    rows_all, cols_all = near.shape[1], near.shape[2]
    table_y, table_x = spectrum_tables(rows_all, cols_all, order)
    half = jnp.einsum("pxy,yb->pxb", near, table_y, precision=lax.Precision.HIGHEST)
    real, imag = half[:, :, :order], half[:, :, order:]
    both = jnp.concatenate(
        (jnp.concatenate((real, imag), axis=2), jnp.concatenate((imag, -real), axis=2)), axis=1
    )
    return jnp.einsum("ax,pxb->pab", table_x, both, precision=lax.Precision.HIGHEST)


def local(
    e_field, h_field, material, permittivity, conductivity, src_shift, src_weight, pupil_mask
):
    depth = e_field.shape[1]
    devices = lax.axis_size("gx") * lax.axis_size("gy")
    keep, drive = coefficients(material, permittivity, conductivity)
    e = e_field
    h = h_field
    for step in range(STEPS):
        upper = passed_along(jnp.stack((e[1][:, :1], e[2][:, :1])), "gx", -1)
        right = passed_along(jnp.stack((e[0][:, :, :1], e[2][:, :, :1])), "gy", -1)
        h = magnetic(e, h, (upper[0], upper[1]), (right[0], right[1]))
        lower = passed_along(jnp.stack((h[1][:, -1:], h[2][:, -1:])), "gx", 1)
        left = passed_along(jnp.stack((h[0][:, :, -1:], h[2][:, :, -1:])), "gy", 1)
        e = electric(e, h, keep, drive, (lower[0], lower[1]), (left[0], left[1]))
    near = e[0:2, depth - 1]
    whole = lax.all_gather(near, ("gx", "gy"))
    whole = whole.reshape((lax.axis_size("gx"), lax.axis_size("gy")) + near.shape)
    whole = whole.transpose(2, 0, 3, 1, 4).reshape(
        2, near.shape[1] * lax.axis_size("gx"), near.shape[2] * lax.axis_size("gy")
    )
    spectrum = exit_spectrum(whole, K).astype(jnp.bfloat16)
    second, first, spread = image_tables(PW, IMG)
    zero = jnp.zeros((), jnp.int32)
    parts = spectrum.reshape(2, K, 2, K)

    def cut(shift):
        return lax.dynamic_slice(parts, (zero, shift[0], zero, shift[1]), (2, PW, 2, PW))

    count = src_shift.shape[0]
    pieces = jax.vmap(cut)(src_shift) * pupil_mask.astype(jnp.bfloat16)[None, None, :, None, :]
    arranged = pieces.reshape(count * 2 * PW, 2 * PW)
    halves = jnp.dot(arranged, second, preferred_element_type=jnp.float32).astype(jnp.bfloat16)
    coarse = IMG // 2
    halves = halves.reshape(count * 2, PW, 2, coarse).transpose(0, 2, 1, 3)
    halves = halves.reshape(count * 2, 2 * PW, coarse)
    factors = jnp.repeat(src_weight / (count * devices), 2)

    def add(total, item):
        field = jnp.dot(first, item[0], preferred_element_type=jnp.float32)
        return (
            total + item[1] * (field[:coarse] * field[:coarse] + field[coarse:] * field[coarse:]),
            None,
        )

    total, _ = lax.scan(add, jnp.zeros((coarse, coarse), jnp.float32), (halves, factors), unroll=4)
    tall = jnp.dot(spread, total, precision=lax.Precision.HIGHEST).astype(jnp.bfloat16)
    blocks = lax.all_to_all(
        tall.reshape(devices, IMG // devices, coarse), ("gx", "gy"), 0, 0, tiled=True
    )
    owned = jnp.sum(blocks.astype(jnp.float32), axis=0)
    image = jnp.dot(owned, spread.T, precision=lax.Precision.HIGHEST)
    return (image, e, h)


def solution(mesh):
    return jax.shard_map(
        local,
        mesh=mesh,
        in_specs=(
            P(None, None, "gx", "gy"),
            P(None, None, "gx", "gy"),
            P(None, "gx", "gy"),
            P(),
            P(),
            P(("gx", "gy"), None),
            P(("gx", "gy")),
            P(),
        ),
        out_specs=(P(("gx", "gy"), None), P(None, None, "gx", "gy"), P(None, None, "gx", "gy")),
        check_vma=False,
    )
```

time: 447 us -> 252 us (0.56)
  waiting for transfers between devices: 134 us -> 11.4 us
  local copies, waits for them, and re-layouts: 92 us -> 63.7 us
  other arithmetic: 71.7 us -> 46 us
  matrix products: 31.2 us -> 9.92 us
  between operations: 15.1 us -> 1.82 us
  blocking collectives: 54.5 us -> 67.1 us
    reduce_scatter x1 -> x0, waiting for transfers between devices: 131 us -> none  [local(): lax.psum_scatter(total, ('gx', 'gy'), scatter_dimension=0, tiled=True)]
    all_gather x0 -> x1, blocking collectives: none -> 67.1 us  [local(): whole = lax.all_gather(near, ('gx', 'gy'))]
    psum x1 -> x0, blocking collectives: 54.5 us -> none  [local(): spectrum_b = lax.psum(partial_value, ('gx', 'gy')).astype(jnp.bfloat16)]
    dot_general x19 -> x21, matrix products: 31.2 us -> 9.92 us  [the longest x16 3.64 us: add(): field = jnp.dot(first, item[0], preferred_element_type=jnp.float32)]
    dynamic_slice x16 -> x4, local copies, waits for them, and re-layouts: 9.42 us -> 0.03 us  [local(): lax.scan(add, jnp.zeros((coarse, coarse), jnp.float32), (halves, factors)...]
    add x19 -> x4, other arithmetic: 20 us -> 11.2 us  [add(): total + item[1] * (field[:coarse] * field[:coarse] + field[coarse:] * fie...]
    all_to_all x0 -> x1, waiting for transfers between devices: none -> 8.81 us  [local(): lax.all_to_all(tall.reshape(devices, IMG // devices, coarse), ('gx', 'gy'...]
    reshape x2 -> x1, local copies, waits for them, and re-layouts: 7.72 us -> 2.1 us  [local(): halves = halves.reshape(count * 2, PW, 2, coarse).transpose(0, 2, 1, 3)]
  transfers between devices with their start and end apart: 17 -> 17, of which waited for: 3 -> 5; matrix products, arithmetic and copies ran while one was open for 16% -> 19% of each run, Pallas kernels for 0% -> 0%
where the time goes in v1:
time: 252 us; the launch traced here: 251 us
  blocking collectives  67.1 us (27%)
  local copies, waits for them, and re-layouts  63.7 us (25%)
  starting transfers between devices  50.2 us (20%)
  other arithmetic  46 us (18%)
  waiting for transfers between devices  11.4 us (5%)
  matrix products  9.92 us (4%)
    all_gather x1, blocking collectives, local(): whole = lax.all_gather(near, ('gx', 'gy'))  67.1 us
    ppermute x16, starting transfers between devices, passed_along(): lax.ppermute(value, axis, [(source, source + steps) for source in range(f...  47.5 us
    gather x40, local copies, waits for them, and re-layouts  18.4 us
    slice x24, local copies, waits for them, and re-layouts, ahead(): lax.slice_in_dim(field, 1, count, axis=axis)  12.8 us
    add x4, other arithmetic, add(): total + item[1] * (field[:coarse] * field[:coarse] + field[coarse:] * fie...  11.2 us
    all_to_all x1, waiting for transfers between devices, local(): lax.all_to_all(tall.reshape(devices, IMG // devices, coarse), ('gx', 'gy'...  8.81 us
    add x3, other arithmetic, electric(): new_x = keep * e[0] + drive * (hz - hz_y - (hy - hy_z))  8.09 us
    squeeze x14, local copies, waits for them, and re-layouts, local(): h = magnetic(e, h, (upper[0], upper[1]), (right[0], right[1]))  7.77 us
  transfers between devices with their start and end apart: 17, of which 5 were waited for; matrix products, arithmetic and copies ran while one was open for 19% of the time, Pallas kernels for 0%

profile of v1, /device:TPU:0, one launch (start us, length us, event | category | flops | bytes accessed | tf_op | source)
XLA Modules:
  0.0 250.5 jit_solution(3206884907036376659)
XLA Ops:
  9.6 6.1 %select_select_fusion = (f32[64,8,128]{2,1,0:T(8,128)S(1)}, pred[64,8,128]{2,1,0:T(8,128)(4,1)S(1)}, pred[64,8,128]{2,1,0:T(8,128)(4,1)S(1)}, pred[64,8,128]{2,1...) fusion(f32[]{:T(128)} %bitcast.17, f32[]{:T(128)} %bitcast.16, ...), kind=kLoop, calls=%fused_computation.178 | loop fusion | flops 1048576 | bytes 1048608 | tf_op jit(solution)/shard_map/jit(_where)/select_n | solution.py:33
  21.6 2.1 fusion.33
  24.3 4.8 %collective-permute-start.2 = (f32[2,64,8,1]{1,2,3,0:T(8,128)S(1)}, f32[2,64,8,1]{1,2,3,0:T(8,128)S(1)}, u32[]{:S(2)}, u32[]{:S(2)}) collective-permute-start(f32[2,64,8,1]{1,2,3,0:T(8,128)S(1)} %pad_maximum_fusion.12), channel_id=1, source_target_pairs={{0,1},{2,3},{4,5},{6,7},{8,9},{10,11},{12,13},{14,15},{16,17},{18,... | collective-permute-start | bytes 12296 | tf_op jit(solution)/shard_map/ppermute | solution.py:21
  31.2 3.4 %collective-permute-start.3 = (f32[2,64,1,128]{3,1,2,0:T(8,128)}, f32[2,64,1,128]{3,1,2,0:T(8,128)}, u32[]{:S(2)}, u32[]{:S(2)}) collective-permute-start(f32[2,64,1,128]{3,1,2,0:T(8,128)} %pad_maximum_fusion.3), channel_id=1, source_target_pairs={{0,2},{2,4},{4,6},{6,8},{8,10},{10,12},{12,14},{14,16},{16,18},{18... | collective-permute-start | bytes 196616 | tf_op jit(solution)/shard_map/ppermute | solution.py:21
  35.0 6.3 %fusion.96 = (f32[64,8,128]{2,1,0:T(8,128)S(1)}, f32[64,8,128]{2,1,0:T(8,128)S(1)}) fusion(f32[64,8,128]{2,0,1:T(8,128)S(1)} %fusion.35, f32[3,64,8,128]{3,2,1,0:T(8,128)S(1)} %copy-done.3, pred[64,8,128]{2,1,0:T(8,128)(4,1)} %get-tuple-element.206, pred[64,8,128]{2,1,0:T(8,128)(4,1)} %get-tuple-element.205, pred[64,8,128]{2,1,0:T(8,128)(4,1)S(1)} %copy-done.22, ...), kind=kLoop, calls=%fused_computation.160 | loop fusion | flops 655360 | bytes 1572896 | tf_op jit(solution)/shard_map/add | solution.py:75
  43.3 2.1 copy_multiply_fusion.1
  56.9 4.3 %collective-permute-start.6 = (f32[2,64,8,1]{1,2,3,0:T(8,128)S(1)}, f32[2,64,8,1]{1,2,3,0:T(8,128)S(1)}, u32[]{:S(2)}, u32[]{:S(2)}) collective-permute-start(f32[2,64,8,1]{1,2,3,0:T(8,128)S(1)} %pad_maximum_fusion.14), channel_id=1, source_target_pairs={{0,1},{2,3},{4,5},{6,7},{8,9},{10,11},{12,13},{14,15},{16,17},{18,... | collective-permute-start | bytes 12296 | tf_op jit(solution)/shard_map/ppermute | solution.py:21
  63.0 4.5 %collective-permute-start.7 = (f32[2,64,1,128]{3,1,2,0:T(8,128)S(1)}, f32[2,64,1,128]{3,1,2,0:T(8,128)S(1)}, u32[]{:S(2)}, u32[]{:S(2)}) collective-permute-start(f32[2,64,1,128]{3,1,2,0:T(8,128)S(1)} %pad_maximum_fusion.5), channel_id=1, source_target_pairs={{0,2},{2,4},{4,6},{6,8},{8,10},{10,12},{12,14},{14,16},{16,18},{18... | collective-permute-start | bytes 196616 | tf_op jit(solution)/shard_map/ppermute | solution.py:21
  81.2 4.2 %collective-permute-start.10 = (f32[2,64,8,1]{1,2,3,0:T(8,128)S(1)}, f32[2,64,8,1]{1,2,3,0:T(8,128)S(1)}, u32[]{:S(2)}, u32[]{:S(2)}) collective-permute-start(f32[2,64,8,1]{1,2,3,0:T(8,128)S(1)} %pad_maximum_fusion.16), channel_id=1, source_target_pairs={{0,1},{2,3},{4,5},{6,7},{8,9},{10,11},{12,13},{14,15},{16,17},{18,... | collective-permute-start | bytes 12296 | tf_op jit(solution)/shard_map/ppermute | solution.py:21
  86.9 5.4 %collective-permute-start.11 = (f32[2,64,1,128]{3,1,2,0:T(8,128)S(1)}, f32[2,64,1,128]{3,1,2,0:T(8,128)S(1)}, u32[]{:S(2)}, u32[]{:S(2)}) collective-permute-start(f32[2,64,1,128]{3,1,2,0:T(8,128)S(1)} %pad_maximum_fusion.7), channel_id=1, source_target_pairs={{0,2},{2,4},{4,6},{6,8},{8,10},{10,12},{12,14},{14,16},{16,18},{18... | collective-permute-start | bytes 196616 | tf_op jit(solution)/shard_map/ppermute | solution.py:21
  106.2 4.5 %collective-permute-start.14 = (f32[2,64,8,1]{1,2,3,0:T(8,128)S(1)}, f32[2,64,8,1]{1,2,3,0:T(8,128)S(1)}, u32[]{:S(2)}, u32[]{:S(2)}) collective-permute-start(f32[2,64,8,1]{1,2,3,0:T(8,128)S(1)} %pad_maximum_fusion.18), channel_id=1, source_target_pairs={{0,1},{2,3},{4,5},{6,7},{8,9},{10,11},{12,13},{14,15},{16,17},{18,... | collective-permute-start | bytes 12296 | tf_op jit(solution)/shard_map/ppermute | solution.py:21
  112.2 6.1 %collective-permute-start.15 = (f32[2,64,1,128]{3,1,2,0:T(8,128)S(1)}, f32[2,64,1,128]{3,1,2,0:T(8,128)S(1)}, u32[]{:S(2)}, u32[]{:S(2)}) collective-permute-start(f32[2,64,1,128]{3,1,2,0:T(8,128)S(1)} %pad_maximum_fusion.9), channel_id=1, source_target_pairs={{0,2},{2,4},{4,6},{6,8},{8,10},{10,12},{12,14},{14,16},{16,18},{18... | collective-permute-start | bytes 196616 | tf_op jit(solution)/shard_map/ppermute | solution.py:21
  119.1 2.2 fusion.95
  121.3 67.1 %all-gather = f32[64,1,8,128]{3,2,1,0:T(8,128)S(1)} all-gather(f32[2,1,8,128]{3,2,1,0:T(8,128)S(1)} %pad_maximum_fusion.10), channel_id=2, replica_groups=mesh['gx'=16,'gy'=2] {'gx','gy'}, dimensions={0}, use_global_device_ids=true | all-gather | bytes 270336 | tf_op jit(solution)/shard_map/all_gather | solution.py:133
  191.0 18.6 %while.13 = (s32[]{:T(128)}, bf16[2,256,2,256]{1,3,2,0:T(8,128)(2,1)S(1)}, s32[8,4]{0,1:T(4,128)S(1)}, bf16[8,2,128,2,128]{4,3,2,1,0:T(2,128)(2,1)S(1)}, s32[]{:T(128)}) while((s32[]{:T(128)}, bf16[2,256,2,256]{1,3,2,0:T(8,128)(2,1)S(1)}, s32[8,4]{0,1:T(4,128)S(1)}, bf16[8,2,128,2,128]{4,3,2,1,0:T(2,128)(2,1)S(1)}, s32[]{:T(128)}) %tuple.151), condition=%wide.while_cond, body=%wide.while_body.sunk | while | flops 2 | bytes 786565 | solution.py:144
  211.2 2.1 reshape.49
  215.3 17.6 %while.14 = (s32[]{:T(128)}, f32[256,256]{1,0:T(8,128)S(1)}, f32[4,4]{1,0:T(4,128)S(1)}, bf16[4,4,256,256]{3,2,1,0:T(8,128)(2,1)S(1)}, s32[]{:T(128)}, /*index=5...) while((s32[]{:T(128)}, f32[256,256]{1,0:T(8,128)S(1)}, ...), condition=%wide.region_1.2_spmd.clone.clone, body=%wide.region_0.1_spmd.sunk.clone.clone.sunk | while | flops 269811712 | bytes 6291723 | solution.py:162
  216.9 2.8 %fusion.149 = f32[256,256]{1,0:T(8,128)S(1)} fusion(f32[512,256]{1,0:T(8,128)S(1)} %fusion.144, f32[512,256]{1,0:T(8,128)S(1)} %fusion.145, f32[512,256]{1,0:T(8,128)S(1)} %fusion.146, f32[512,256]{1,0:T(8,128)S(1)} %fusion.147, f32[256,256]{1,0:T(8,128)S(1)} %get-tuple-element.387, f32[]{:T(128)} %bitcast.288, f32[]{:T(128)} %bitcast.289, ...), kind=kLoop, calls=%fused_computation.6.clone.1 | loop fusion | flops 1376256 | bytes 2621457 | tf_op jit(solution)/shard_map/while/body/eval_jaxpr/add | solution.py:158
  221.4 2.8 %fusion.149 = f32[256,256]{1,0:T(8,128)S(1)} fusion(f32[512,256]{1,0:T(8,128)S(1)} %fusion.144, f32[512,256]{1,0:T(8,128)S(1)} %fusion.145, f32[512,256]{1,0:T(8,128)S(1)} %fusion.146, f32[512,256]{1,0:T(8,128)S(1)} %fusion.147, f32[256,256]{1,0:T(8,128)S(1)} %get-tuple-element.387, f32[]{:T(128)} %bitcast.288, f32[]{:T(128)} %bitcast.289, ...), kind=kLoop, calls=%fused_computation.6.clone.1 | loop fusion | flops 1376256 | bytes 2621457 | tf_op jit(solution)/shard_map/while/body/eval_jaxpr/add | solution.py:158
  225.8 2.8 %fusion.149 = f32[256,256]{1,0:T(8,128)S(1)} fusion(f32[512,256]{1,0:T(8,128)S(1)} %fusion.144, f32[512,256]{1,0:T(8,128)S(1)} %fusion.145, f32[512,256]{1,0:T(8,128)S(1)} %fusion.146, f32[512,256]{1,0:T(8,128)S(1)} %fusion.147, f32[256,256]{1,0:T(8,128)S(1)} %get-tuple-element.387, f32[]{:T(128)} %bitcast.288, f32[]{:T(128)} %bitcast.289, ...), kind=kLoop, calls=%fused_computation.6.clone.1 | loop fusion | flops 1376256 | bytes 2621457 | tf_op jit(solution)/shard_map/while/body/eval_jaxpr/add | solution.py:158
  230.2 2.8 %fusion.149 = f32[256,256]{1,0:T(8,128)S(1)} fusion(f32[512,256]{1,0:T(8,128)S(1)} %fusion.144, f32[512,256]{1,0:T(8,128)S(1)} %fusion.145, f32[512,256]{1,0:T(8,128)S(1)} %fusion.146, f32[512,256]{1,0:T(8,128)S(1)} %fusion.147, f32[256,256]{1,0:T(8,128)S(1)} %get-tuple-element.387, f32[]{:T(128)} %bitcast.288, f32[]{:T(128)} %bitcast.289, ...), kind=kLoop, calls=%fused_computation.6.clone.1 | loop fusion | flops 1376256 | bytes 2621457 | tf_op jit(solution)/shard_map/while/body/eval_jaxpr/add | solution.py:158
  233.0 2.2 fusion.20
  236.1 2.7 %all-to-all-start = ((bf16[32,16,256]{2,1,0:T(8,128)(2,1)}), bf16[32,16,256]{2,1,0:T(8,128)(2,1)S(1)}, u32[]{:S(2)}, u32[]{:S(2)}) async-start(bf16[32,16,256]{2,1,0:T(8,128)(2,1)} %bitcast.96), calls=%async_computation | async-start | bytes 524288 | tf_op jit(solution)/shard_map/all_to_all | solution.py:164
  240.7 8.8 %all-to-all-done = bf16[32,16,256]{2,1,0:T(8,128)(2,1)S(1)} async-done(((bf16[32,16,256]{2,1,0:T(8,128)(2,1)}), bf16[32,16,256]{2,1,0:T(8,128)(2,1)S(1)}, u32[]{:S(2)}, u32[]{:S(2)}) %all-to-all-start) | async-done | bytes 262176 | tf_op jit(solution)/shard_map/all_to_all | solution.py:164
  (309 shorter events, 98.3 us)
Async XLA Ops:
  3.0 16.2 %collective-permute-start.1 = (f32[2,64,8,1]{1,2,3,0:T(8,128)}, f32[2,64,8,1]{1,2,3,0:T(8,128)S(1)}, u32[]{:S(2)}, u32[]{:S(2)}) collective-permute-start(f32[2,64,8,1]{1,2,3,0:T(8,128)} %pad_maximum_fusion.11), channel_id=1, source_target_pairs={{1,0},{3,2},{5,4},{7,6},{9,8},{11,10},{13,12},{15,14},{17,16},{19,... | collective-permute-start | bytes 12296 | tf_op jit(solution)/shard_map/ppermute | solution.py:21
  5.0 15.9 %collective-permute-start = (f32[2,64,1,128]{3,1,2,0:T(8,128)}, f32[2,64,1,128]{3,1,2,0:T(8,128)}, u32[]{:S(2)}, u32[]{:S(2)}) collective-permute-start(f32[2,64,1,128]{3,1,2,0:T(8,128)} %pad_maximum_fusion.2), channel_id=1, source_target_pairs={{2,0},{4,2},{6,4},{8,6},{10,8},{12,10},{14,12},{16,14},{18,16},{20... | collective-permute-start | bytes 196616 | tf_op jit(solution)/shard_map/ppermute | solution.py:21
  24.3 10.3 %collective-permute-start.2 = (f32[2,64,8,1]{1,2,3,0:T(8,128)S(1)}, f32[2,64,8,1]{1,2,3,0:T(8,128)S(1)}, u32[]{:S(2)}, u32[]{:S(2)}) collective-permute-start(f32[2,64,8,1]{1,2,3,0:T(8,128)S(1)} %pad_maximum_fusion.12), channel_id=1, source_target_pairs={{0,1},{2,3},{4,5},{6,7},{8,9},{10,11},{12,13},{14,15},{16,17},{18,... | collective-permute-start | bytes 12296 | tf_op jit(solution)/shard_map/ppermute | solution.py:21
  31.2 11.3 %collective-permute-start.3 = (f32[2,64,1,128]{3,1,2,0:T(8,128)}, f32[2,64,1,128]{3,1,2,0:T(8,128)}, u32[]{:S(2)}, u32[]{:S(2)}) collective-permute-start(f32[2,64,1,128]{3,1,2,0:T(8,128)} %pad_maximum_fusion.3), channel_id=1, source_target_pairs={{0,2},{2,4},{4,6},{6,8},{8,10},{10,12},{12,14},{14,16},{16,18},{18... | collective-permute-start | bytes 196616 | tf_op jit(solution)/shard_map/ppermute | solution.py:21
  45.6 5.6 %collective-permute-start.5 = (f32[2,64,8,1]{1,2,3,0:T(8,128)S(1)}, f32[2,64,8,1]{1,2,3,0:T(8,128)S(1)}, u32[]{:S(2)}, u32[]{:S(2)}) collective-permute-start(f32[2,64,8,1]{1,2,3,0:T(8,128)S(1)} %pad_maximum_fusion.13), channel_id=1, source_target_pairs={{1,0},{3,2},{5,4},{7,6},{9,8},{11,10},{13,12},{15,14},{17,16},{19,... | collective-permute-start | bytes 12296 | tf_op jit(solution)/shard_map/ppermute | solution.py:21
  50.0 4.6 %collective-permute-start.4 = (f32[2,64,1,128]{3,1,2,0:T(8,128)S(1)}, f32[2,64,1,128]{3,1,2,0:T(8,128)S(1)}, u32[]{:S(2)}, u32[]{:S(2)}) collective-permute-start(f32[2,64,1,128]{3,1,2,0:T(8,128)S(1)} %pad_maximum_fusion.4), channel_id=1, source_target_pairs={{2,0},{4,2},{6,4},{8,6},{10,8},{12,10},{14,12},{16,14},{18,16},{20... | collective-permute-start | bytes 196616 | tf_op jit(solution)/shard_map/ppermute | solution.py:21
  56.9 10.7 %collective-permute-start.6 = (f32[2,64,8,1]{1,2,3,0:T(8,128)S(1)}, f32[2,64,8,1]{1,2,3,0:T(8,128)S(1)}, u32[]{:S(2)}, u32[]{:S(2)}) collective-permute-start(f32[2,64,8,1]{1,2,3,0:T(8,128)S(1)} %pad_maximum_fusion.14), channel_id=1, source_target_pairs={{0,1},{2,3},{4,5},{6,7},{8,9},{10,11},{12,13},{14,15},{16,17},{18,... | collective-permute-start | bytes 12296 | tf_op jit(solution)/shard_map/ppermute | solution.py:21
  63.0 5.6 %collective-permute-start.7 = (f32[2,64,1,128]{3,1,2,0:T(8,128)S(1)}, f32[2,64,1,128]{3,1,2,0:T(8,128)S(1)}, u32[]{:S(2)}, u32[]{:S(2)}) collective-permute-start(f32[2,64,1,128]{3,1,2,0:T(8,128)S(1)} %pad_maximum_fusion.5), channel_id=1, source_target_pairs={{0,2},{2,4},{4,6},{6,8},{8,10},{10,12},{12,14},{14,16},{16,18},{18... | collective-permute-start | bytes 196616 | tf_op jit(solution)/shard_map/ppermute | solution.py:21
  71.2 5.6 %collective-permute-start.9 = (f32[2,64,8,1]{1,2,3,0:T(8,128)S(1)}, f32[2,64,8,1]{1,2,3,0:T(8,128)S(1)}, u32[]{:S(2)}, u32[]{:S(2)}) collective-permute-start(f32[2,64,8,1]{1,2,3,0:T(8,128)S(1)} %pad_maximum_fusion.15), channel_id=1, source_target_pairs={{1,0},{3,2},{5,4},{7,6},{9,8},{11,10},{13,12},{15,14},{17,16},{19,... | collective-permute-start | bytes 12296 | tf_op jit(solution)/shard_map/ppermute | solution.py:21
  75.0 3.4 %collective-permute-start.8 = (f32[2,64,1,128]{3,1,2,0:T(8,128)S(1)}, f32[2,64,1,128]{3,1,2,0:T(8,128)S(1)}, u32[]{:S(2)}, u32[]{:S(2)}) collective-permute-start(f32[2,64,1,128]{3,1,2,0:T(8,128)S(1)} %pad_maximum_fusion.6), channel_id=1, source_target_pairs={{2,0},{4,2},{6,4},{8,6},{10,8},{12,10},{14,12},{16,14},{18,16},{20... | collective-permute-start | bytes 196616 | tf_op jit(solution)/shard_map/ppermute | solution.py:21
  81.2 11.1 %collective-permute-start.10 = (f32[2,64,8,1]{1,2,3,0:T(8,128)S(1)}, f32[2,64,8,1]{1,2,3,0:T(8,128)S(1)}, u32[]{:S(2)}, u32[]{:S(2)}) collective-permute-start(f32[2,64,8,1]{1,2,3,0:T(8,128)S(1)} %pad_maximum_fusion.16), channel_id=1, source_target_pairs={{0,1},{2,3},{4,5},{6,7},{8,9},{10,11},{12,13},{14,15},{16,17},{18,... | collective-permute-start | bytes 12296 | tf_op jit(solution)/shard_map/ppermute | solution.py:21
  86.9 6.4 %collective-permute-start.11 = (f32[2,64,1,128]{3,1,2,0:T(8,128)S(1)}, f32[2,64,1,128]{3,1,2,0:T(8,128)S(1)}, u32[]{:S(2)}, u32[]{:S(2)}) collective-permute-start(f32[2,64,1,128]{3,1,2,0:T(8,128)S(1)} %pad_maximum_fusion.7), channel_id=1, source_target_pairs={{0,2},{2,4},{4,6},{6,8},{8,10},{10,12},{12,14},{14,16},{16,18},{18... | collective-permute-start | bytes 196616 | tf_op jit(solution)/shard_map/ppermute | solution.py:21
  95.3 6.5 %collective-permute-start.13 = (f32[2,64,8,1]{1,2,3,0:T(8,128)S(1)}, f32[2,64,8,1]{1,2,3,0:T(8,128)S(1)}, u32[]{:S(2)}, u32[]{:S(2)}) collective-permute-start(f32[2,64,8,1]{1,2,3,0:T(8,128)S(1)} %pad_maximum_fusion.17), channel_id=1, source_target_pairs={{1,0},{3,2},{5,4},{7,6},{9,8},{11,10},{13,12},{15,14},{17,16},{19,... | collective-permute-start | bytes 12296 | tf_op jit(solution)/shard_map/ppermute | solution.py:21
  100.5 3.2 %collective-permute-start.12 = (f32[2,64,1,128]{3,1,2,0:T(8,128)S(1)}, f32[2,64,1,128]{3,1,2,0:T(8,128)S(1)}, u32[]{:S(2)}, u32[]{:S(2)}) collective-permute-start(f32[2,64,1,128]{3,1,2,0:T(8,128)S(1)} %pad_maximum_fusion.8), channel_id=1, source_target_pairs={{2,0},{4,2},{6,4},{8,6},{10,8},{12,10},{14,12},{16,14},{18,16},{20... | collective-permute-start | bytes 196616 | tf_op jit(solution)/shard_map/ppermute | solution.py:21
  105.5 15.8 %copy-start.1 = (f32[64,8,128]{2,1,0:T(8,128)}, f32[64,8,128]{2,1,0:T(8,128)S(1)}, u32[]{:S(2)}) copy-start(f32[64,8,128]{2,1,0:T(8,128)S(1)} %get-tuple-element.234) | copy-start | bytes 786436
  106.2 12.1 %collective-permute-start.14 = (f32[2,64,8,1]{1,2,3,0:T(8,128)S(1)}, f32[2,64,8,1]{1,2,3,0:T(8,128)S(1)}, u32[]{:S(2)}, u32[]{:S(2)}) collective-permute-start(f32[2,64,8,1]{1,2,3,0:T(8,128)S(1)} %pad_maximum_fusion.18), channel_id=1, source_target_pairs={{0,1},{2,3},{4,5},{6,7},{8,9},{10,11},{12,13},{14,15},{16,17},{18,... | collective-permute-start | bytes 12296 | tf_op jit(solution)/shard_map/ppermute | solution.py:21
  112.2 6.9 %collective-permute-start.15 = (f32[2,64,1,128]{3,1,2,0:T(8,128)S(1)}, f32[2,64,1,128]{3,1,2,0:T(8,128)S(1)}, u32[]{:S(2)}, u32[]{:S(2)}) collective-permute-start(f32[2,64,1,128]{3,1,2,0:T(8,128)S(1)} %pad_maximum_fusion.9), channel_id=1, source_target_pairs={{0,2},{2,4},{4,6},{6,8},{8,10},{10,12},{12,14},{14,16},{16,18},{18... | collective-permute-start | bytes 196616 | tf_op jit(solution)/shard_map/ppermute | solution.py:21
  119.1 69.3 %copy-start.17 = (f32[256,512,1]{1,0,2:T(8,128)S(1)}, f32[256,512,1]{1,0,2:T(8,128)}, u32[]{:S(2)}) copy-start(f32[256,512,1]{1,0,2:T(8,128)} %constant.115) | copy-start | bytes 1572868
  121.3 67.8 %copy-start.4 = (f32[1,64,8,128]{3,2,1,0:T(8,128)}, f32[1,64,8,128]{3,2,1,0:T(8,128)S(1)}, u32[]{:S(2)}) copy-start(f32[1,64,8,128]{3,2,1,0:T(8,128)S(1)} %get-tuple-element.214) | copy-start | bytes 786436
  121.3 69.6 %copy-start.6 = (f32[1,64,8,128]{3,2,1,0:T(8,128)}, f32[1,64,8,128]{3,2,1,0:T(8,128)S(1)}, u32[]{:S(2)}) copy-start(f32[1,64,8,128]{3,2,1,0:T(8,128)S(1)} %get-tuple-element.215) | copy-start | bytes 786436
  121.3 67.8 %copy-start.18 = (f32[256,256,1]{1,0,2:T(8,128)S(1)}, f32[256,256,1]{1,0,2:T(8,128)}, u32[]{:S(2)}) copy-start(f32[256,256,1]{1,0,2:T(8,128)} %constant.116) | copy-start | bytes 786436
  190.9 18.6 %copy-start.25 = (bf16[128,128]{1,0:T(8,128)(2,1)S(1)}, bf16[128,128]{1,0:T(8,128)(2,1)}, u32[]{:S(2)}) copy-start(bf16[128,128]{1,0:T(8,128)(2,1)} %convert_element_type.23) | copy-start | bytes 98308
  236.1 13.5 %copy-start.16 = (f32[256,512]{1,0:T(8,128)S(1)}, f32[256,512]{1,0:T(8,128)}, u32[]{:S(2)}) copy-start(f32[256,512]{1,0:T(8,128)} %constant.62.clone) | copy-start | bytes 1572868
  236.1 13.4 %all-to-all-start = ((bf16[32,16,256]{2,1,0:T(8,128)(2,1)}), bf16[32,16,256]{2,1,0:T(8,128)(2,1)S(1)}, u32[]{:S(2)}, u32[]{:S(2)}) async-start(bf16[32,16,256]{2,1,0:T(8,128)(2,1)} %bitcast.96), calls=%async_computation | async-start | bytes 524288 | tf_op jit(solution)/shard_map/all_to_all | solution.py:164
  (23 other events, 123.2 us)

commit v2 on v1

v2 whole, which is shorter than its diff:
```python
import functools

import jax
import jax.numpy as jnp
import numpy as np
from jax import lax
from jax.experimental import pallas as pl
from jax.experimental.pallas import tpu as pltpu
from jax.sharding import PartitionSpec as P

STEPS = 4
K = 256
PW = 128
IMG = 512
COURANT = 0.5
MESH = pl.DeviceIdType.MESH
HIGHEST = lax.Precision.HIGHEST
VMEM = pl.BlockSpec(memory_space=pltpu.VMEM)
SMEM = pl.BlockSpec(memory_space=pltpu.SMEM)
ANY = pl.BlockSpec(memory_space=pl.ANY)


def spectrum_tables(rows_all, cols_all, order):
    freqs = np.arange(order) - order // 2
    phase_y = 2.0 * np.pi * np.mod(np.arange(cols_all)[:, None] * freqs[None, :], cols_all) / cols_all
    table_y = np.concatenate((np.cos(phase_y), -np.sin(phase_y)), axis=1)
    phase_x = 2.0 * np.pi * np.mod(freqs[:, None] * np.arange(rows_all)[None, :], rows_all) / rows_all
    table_x = np.concatenate((np.cos(phase_x), np.sin(phase_x)), axis=1) / np.sqrt(rows_all * cols_all)
    return table_y.astype(np.float32), table_x.astype(np.float32)


def image_tables(window, pixels):
    coarse = pixels // 2
    offsets = np.arange(window) - window // 2
    phase = 2.0 * np.pi * np.mod(offsets[:, None] * np.arange(coarse)[None, :], coarse) / coarse
    cosine, sine = np.cos(phase), np.sin(phase)
    second = np.block([[cosine, sine], [-sine, cosine]])
    first = np.block([[cosine.T, -sine.T], [sine.T, cosine.T]]) / window
    gaps = np.arange(pixels)[:, None] - 2 * np.arange(coarse)[None, :]
    spread = np.ones(gaps.shape)
    for order in range(1, coarse // 2):
        spread += 2.0 * np.cos(2.0 * np.pi * np.mod(order * gaps, pixels) / pixels)
    spread += np.cos(np.pi * gaps / 2.0)
    spread = spread / coarse
    return second.astype(jnp.bfloat16), first.astype(jnp.bfloat16), spread.astype(np.float32)


def greet_all(nx, ny, me):
    barrier = pltpu.get_barrier_semaphore()

    def greet(step, carry):
        other = lax.rem(me + step, nx * ny)
        pl.semaphore_signal(
            barrier, inc=1, device_id=(other // ny, lax.rem(other, ny)), device_id_type=MESH
        )
        return carry

    lax.fori_loop(1, nx * ny, greet, 0)
    pl.semaphore_wait(barrier, nx * ny - 1)


def fields_kernel(
    nx, ny, perm, cond, e_in, h_in, mat_in, e_out, h_out, near,
    e, h, mat, keep, drive, edge_x, face_x, face_y, got_x, got_y, in_sem, x_send, x_recv, y_send, y_recv,
    n_send, n_recv,
):
    depth = mat.shape[0]
    rows, cols = mat.shape[1], mat.shape[2]
    gx, gy = lax.axis_index("gx"), lax.axis_index("gy")
    me = gx * ny + gy
    loads = (
        pltpu.make_async_copy(e_in, e.at[:, pl.ds(0, depth)], in_sem.at[0]),
        pltpu.make_async_copy(h_in, h.at[:, pl.ds(1, depth)], in_sem.at[1]),
        pltpu.make_async_copy(mat_in, mat, in_sem.at[2]),
    )
    for load in loads:
        load.start()
    got_x[...] = jnp.zeros_like(got_x)
    got_y[...] = jnp.zeros_like(got_y)
    greet_all(nx, ny, me)
    zero = jnp.zeros((rows, cols), jnp.float32)
    for c in range(3):
        e[c, depth] = zero
        h[c, 0] = zero
    lane = lax.broadcasted_iota(jnp.int32, (rows, cols), 1)
    row = lax.broadcasted_iota(jnp.int32, (rows, cols), 0)
    keeps, drives = [], []
    for m in range(perm.shape[0]):
        loss = cond[m] / (2.0 * perm[m])
        keeps.append((1.0 - loss) / (1.0 + loss))
        drives.append(COURANT / (perm[m] * (1.0 + loss)))

    def x_copy(turn):
        to = gx - 1 if turn % 2 == 0 else gx + 1
        return pltpu.make_async_remote_copy(
            src_ref=face_x.at[turn], dst_ref=got_x.at[turn], send_sem=x_send.at[turn],
            recv_sem=x_recv.at[turn], device_id=(to, gy), device_id_type=MESH,
        )

    def y_copy(turn):
        to = gy - 1 if turn % 2 == 0 else gy + 1
        return pltpu.make_async_remote_copy(
            src_ref=face_y.at[turn], dst_ref=got_y.at[turn], send_sem=y_send.at[turn],
            recv_sem=y_recv.at[turn], device_id=(gx, to), device_id_type=MESH,
        )

    def sends(turn):
        if turn % 2 == 0:
            return gx > 0, gy > 0
        return gx < nx - 1, gy < ny - 1

    def gets(turn):
        if turn % 2 == 0:
            return gx < nx - 1, gy < ny - 1
        return gx > 0, gy > 0

    def start(turn):
        field, base, edge, first, second = (e, 0, 0, 0, 2) if turn % 2 == 0 else (h, 1, cols - 1, 0, 2)
        at_row = 0 if turn % 2 == 0 else rows - 1
        x_to, y_to = sends(turn)
        for k, c in enumerate((1, 2)):
            face_x[turn, k] = field[c, pl.ds(base, depth), at_row, :].astype(jnp.bfloat16)

        @pl.when(x_to)
        def _():
            x_copy(turn).start()

        def pack(z, face):
            for k, c in enumerate((first, second)):
                spot = k * depth + z
                moved = pltpu.roll(field[c, base + z], lax.rem(spot - edge + cols, cols), 1)
                face = jnp.where(lane == spot, moved, face)
            return face

        face_y[turn] = lax.fori_loop(0, depth, pack, zero, unroll=8)

        @pl.when(y_to)
        def _():
            y_copy(turn).start()

    def arrive(turn):
        x_from, y_from = gets(turn)

        @pl.when(y_from)
        def _():
            y_copy(turn).wait_recv()

        @pl.when(x_from)
        def _():
            x_copy(turn).wait_recv()

    def magnetic(turn):
        face = got_y[turn]
        edge_x[...] = got_x[turn].astype(jnp.float32)

        def at(z, carry):
            ex, ey, ez = e[0, z], e[1, z], e[2, z]
            ex_z, ey_z = e[0, z + 1], e[1, z + 1]
            last_row, last_lane = row == rows - 1, lane == cols - 1
            ey_f = edge_x[0, pl.ds(z, 1), :]
            ez_f = edge_x[1, pl.ds(z, 1), :]
            ex_f = pltpu.roll(face, cols - 1 - z, 1)
            ez_g = pltpu.roll(face, cols - 1 - depth - z, 1)
            ey_x = jnp.where(last_row, ey_f, pltpu.roll(ey, rows - 1, 0))
            ez_x = jnp.where(last_row, ez_f, pltpu.roll(ez, rows - 1, 0))
            ex_y = jnp.where(last_lane, ex_f, pltpu.roll(ex, cols - 1, 1))
            ez_y = jnp.where(last_lane, ez_g, pltpu.roll(ez, cols - 1, 1))
            h[0, z + 1] = h[0, z + 1] - COURANT * (ez_y - ez - (ey_z - ey))
            h[1, z + 1] = h[1, z + 1] - COURANT * (ex_z - ex - (ez_x - ez))
            h[2, z + 1] = h[2, z + 1] - COURANT * (ey_x - ey - (ex_y - ex))
            return carry

        lax.fori_loop(0, depth, at, 0, unroll=8)

    def electric(turn):
        face = got_y[turn]
        edge_x[...] = got_x[turn].astype(jnp.float32)

        def at(z, carry):
            hx, hy, hz = h[0, z + 1], h[1, z + 1], h[2, z + 1]
            hx_z, hy_z = h[0, z], h[1, z]
            first_row, first_lane = row == 0, lane == 0
            hy_f = edge_x[0, pl.ds(z, 1), :]
            hz_f = edge_x[1, pl.ds(z, 1), :]
            hx_f = pltpu.roll(face, lax.rem(cols - z, cols), 1)
            hz_g = pltpu.roll(face, cols - depth - z, 1)
            hy_x = jnp.where(first_row, hy_f, pltpu.roll(hy, 1, 0))
            hz_x = jnp.where(first_row, hz_f, pltpu.roll(hz, 1, 0))
            hx_y = jnp.where(first_lane, hx_f, pltpu.roll(hx, 1, 1))
            hz_y = jnp.where(first_lane, hz_g, pltpu.roll(hz, 1, 1))
            kept, driven = keep[z], drive[z]
            e[0, z] = kept * e[0, z] + driven * (hz - hz_y - (hy - hy_z))
            e[1, z] = kept * e[1, z] + driven * (hx - hx_z - (hz - hz_x))
            e[2, z] = kept * e[2, z] + driven * (hy - hy_x - (hx - hx_y))
            return carry

        lax.fori_loop(0, depth, at, 0, unroll=8)

    loads[0].wait()
    start(0)
    loads[2].wait()

    def look_up(z, carry):
        index = mat[z]
        kept, driven = zero, zero
        for m in range(len(keeps)):
            chosen = index == m
            kept = jnp.where(chosen, keeps[m], kept)
            driven = jnp.where(chosen, drives[m], driven)
        keep[z] = kept
        drive[z] = driven
        return carry

    lax.fori_loop(0, depth, look_up, 0, unroll=4)
    loads[1].wait()
    for turn in range(2 * STEPS):
        if turn:
            start(turn)
        arrive(turn)
        if turn % 2 == 0:
            magnetic(turn)
        else:
            electric(turn)

    store_h = pltpu.make_async_copy(h.at[:, pl.ds(1, depth)], h_out, in_sem.at[1])
    store_e = pltpu.make_async_copy(e.at[:, pl.ds(0, depth)], e_out, in_sem.at[0])
    store_h.start()
    store_e.start()

    def spot(index):
        x_at = pl.multiple_of((index // ny) * rows, rows)
        y_at = pl.multiple_of(lax.rem(index, ny) * cols, cols)
        return near.at[:, pl.ds(x_at, rows), pl.ds(y_at, cols)]

    def near_copy(step, other, place):
        return pltpu.make_async_remote_copy(
            src_ref=e.at[pl.ds(0, 2), depth - 1], dst_ref=spot(place), send_sem=n_send.at[step],
            recv_sem=n_recv.at[step], device_id=(other // ny, lax.rem(other, ny)), device_id_type=MESH,
        )

    def push(step, carry):
        near_copy(step, lax.rem(me + step, nx * ny), me).start()
        return carry

    lax.fori_loop(1, nx * ny, push, 0)
    own = pltpu.make_async_copy(e.at[pl.ds(0, 2), depth - 1], spot(me), n_send.at[0])
    own.start()
    own.wait()

    def take(step, carry):
        copy = near_copy(
            step, lax.rem(me + step, nx * ny), lax.rem(me - step + nx * ny, nx * ny)
        )
        copy.wait_recv()
        copy.wait_send()
        return carry

    lax.fori_loop(1, nx * ny, take, 0)
    for turn in range(2 * STEPS):
        x_to, y_to = sends(turn)

        @pl.when(x_to)
        def _():
            x_copy(turn).wait_send()

        @pl.when(y_to)
        def _():
            y_copy(turn).wait_send()

    store_h.wait()
    store_e.wait()


def run_fields(e_field, h_field, material, permittivity, conductivity, nx, ny):
    _, depth, rows, cols = e_field.shape
    devices, turns = nx * ny, 2 * STEPS
    f32, dma = jnp.float32, pltpu.SemaphoreType.DMA
    return pl.pallas_call(
        functools.partial(fields_kernel, nx, ny),
        out_shape=(
            jax.ShapeDtypeStruct(e_field.shape, f32),
            jax.ShapeDtypeStruct(h_field.shape, f32),
            jax.ShapeDtypeStruct((2, rows * nx, cols * ny), f32),
        ),
        in_specs=[SMEM, SMEM, ANY, ANY, ANY],
        out_specs=(ANY, ANY, VMEM),
        scratch_shapes=[
            pltpu.VMEM((3, depth + 1, rows, cols), f32),
            pltpu.VMEM((3, depth + 1, rows, cols), f32),
            pltpu.VMEM((depth, rows, cols), jnp.int32),
            pltpu.VMEM((depth, rows, cols), f32),
            pltpu.VMEM((depth, rows, cols), f32),
            pltpu.VMEM((2, depth, cols), f32),
            pltpu.VMEM((turns, 2, depth, cols), jnp.bfloat16),
            pltpu.VMEM((turns, rows, cols), f32),
            pltpu.VMEM((turns, 2, depth, cols), jnp.bfloat16),
            pltpu.VMEM((turns, rows, cols), f32),
            dma((3,)), dma((turns,)), dma((turns,)), dma((turns,)), dma((turns,)),
            dma((devices,)), dma((devices,)),
        ],
        compiler_params=pltpu.CompilerParams(
            collective_id=0, has_side_effects=True, vmem_limit_bytes=40 * 2**20
        ),
        name="fields",
    )(permittivity, conductivity, e_field, h_field, material)


def image_kernel(
    shift, factor, near, table_y, table_x, mask, second, first, spread, tall, spec, total
):
    pols, order = near.shape[0], table_x.shape[0]
    window, coarse = mask.shape[0], spread.shape[1]
    for p in range(pols):
        half = jnp.dot(near[p], table_y[...], precision=HIGHEST, preferred_element_type=jnp.float32)
        real, imag = half[:, :order], half[:, order:]
        both = jnp.concatenate(
            (jnp.concatenate((real, imag), axis=1), jnp.concatenate((imag, -real), axis=1)), axis=0
        )
        value = jnp.dot(table_x[...], both, precision=HIGHEST, preferred_element_type=jnp.float32)
        value = value.astype(jnp.bfloat16).astype(jnp.float32)
        for t in range(spec.shape[1]):
            spec[p, t] = value[:, t * window:(t + 1) * window]
    total[...] = jnp.zeros_like(total)
    keep = mask[...].astype(jnp.float32)

    def add(s, carry):
        a, b = shift[s, 0], shift[s, 1]
        turn = lax.rem(order - b, order)
        pieces = []
        for p in range(pols):
            parts = []
            for k in range(2):
                strip = jnp.concatenate(
                    [
                        spec[p, t, pl.ds(a, window), :]
                        for t in range(k * order // window, (k + 1) * order // window)
                    ],
                    axis=1,
                )
                parts.append(pltpu.roll(strip, turn, 1)[:, :window] * keep)
            pieces.append(jnp.concatenate(parts, axis=1))
        cut = jnp.concatenate(pieces, axis=0).astype(jnp.bfloat16)
        half = jnp.dot(cut, second[...], preferred_element_type=jnp.float32).astype(jnp.bfloat16)
        sides = []
        for p in range(pols):
            part = half[p * window:(p + 1) * window]
            sides.append(jnp.concatenate((part[:, :coarse], part[:, coarse:]), axis=0))
        field = jnp.dot(
            first[...], jnp.concatenate(sides, axis=1), preferred_element_type=jnp.float32
        )
        power = field * field
        power = power[:coarse] + power[coarse:]
        power = sum(power[:, p * coarse:(p + 1) * coarse] for p in range(pols))
        total[...] += factor[s] * power
        return carry

    lax.fori_loop(0, shift.shape[0], add, 0)
    tall[...] = jnp.dot(
        spread[...], total[...], precision=HIGHEST, preferred_element_type=jnp.float32
    ).astype(jnp.bfloat16).reshape(tall.shape)


def run_image(src_shift, factors, near, pupil_mask, devices):
    rows_all, cols_all = near.shape[1], near.shape[2]
    table_y, table_x = spectrum_tables(rows_all, cols_all, K)
    second, first, spread = image_tables(PW, IMG)
    tall = pl.pallas_call(
        image_kernel,
        out_shape=jax.ShapeDtypeStruct((IMG, IMG // 2), jnp.bfloat16),
        in_specs=[SMEM, SMEM] + [VMEM] * 7,
        out_specs=VMEM,
        scratch_shapes=[
            pltpu.VMEM((2, 2 * K // PW, K, PW), jnp.float32),
            pltpu.VMEM((IMG // 2, IMG // 2), jnp.float32),
        ],
        compiler_params=pltpu.CompilerParams(vmem_limit_bytes=40 * 2**20),
        name="sources",
    )(src_shift, factors, near, table_y, table_x, pupil_mask, second, first, spread)
    return tall.reshape(devices, IMG // devices, IMG // 2), spread


def reduce_kernel(nx, ny, tall, spread, image, got, send, recv):
    devices = nx * ny
    me = lax.axis_index("gx") * ny + lax.axis_index("gy")
    greet_all(nx, ny, me)

    def copy(step, other):
        return pltpu.make_async_remote_copy(
            src_ref=tall.at[other], dst_ref=got.at[step], send_sem=send.at[step],
            recv_sem=recv.at[step], device_id=(other // ny, lax.rem(other, ny)), device_id_type=MESH,
        )

    def push(step, carry):
        copy(step, lax.rem(me + step, devices)).start()
        return carry

    lax.fori_loop(1, devices, push, 0)

    def take(step, total):
        arrived = copy(step, lax.rem(me + step, devices))
        arrived.wait_recv()
        arrived.wait_send()
        return total + got[step].astype(jnp.float32)

    owned = lax.fori_loop(1, devices, take, tall[me].astype(jnp.float32))
    image[...] = jnp.dot(owned, spread[...], precision=HIGHEST, preferred_element_type=jnp.float32)


def run_reduce(tall, spread, nx, ny):
    devices = nx * ny
    return pl.pallas_call(
        functools.partial(reduce_kernel, nx, ny),
        out_shape=jax.ShapeDtypeStruct((tall.shape[1], spread.shape[0]), jnp.float32),
        in_specs=[VMEM, VMEM],
        out_specs=VMEM,
        scratch_shapes=[
            pltpu.VMEM(tall.shape, jnp.bfloat16),
            pltpu.SemaphoreType.DMA((devices,)),
            pltpu.SemaphoreType.DMA((devices,)),
        ],
        compiler_params=pltpu.CompilerParams(
            collective_id=1, has_side_effects=True, vmem_limit_bytes=40 * 2**20
        ),
        name="reduce",
    )(tall, np.ascontiguousarray(spread.T))


def local(
    e_field, h_field, material, permittivity, conductivity, src_shift, src_weight, pupil_mask
):
    nx, ny = lax.axis_size("gx"), lax.axis_size("gy")
    devices = nx * ny
    e, h, near = run_fields(e_field, h_field, material, permittivity, conductivity, nx, ny)
    factors = src_weight / (src_shift.shape[0] * devices)
    tall, spread = run_image(src_shift, factors, near, pupil_mask, devices)
    image = run_reduce(tall, spread, nx, ny)
    return (image, e, h)


def solution(mesh):
    return jax.shard_map(
        local,
        mesh=mesh,
        in_specs=(
            P(None, None, "gx", "gy"),
            P(None, None, "gx", "gy"),
            P(None, "gx", "gy"),
            P(),
            P(),
            P(("gx", "gy"), None),
            P(("gx", "gy")),
            P(),
        ),
        out_specs=(P(("gx", "gy"), None), P(None, None, "gx", "gy"), P(None, None, "gx", "gy")),
        check_vma=False,
    )
```

time: 252 us -> 76.3 us (0.30)
  blocking collectives: 67.1 us -> 0 us
  Pallas kernels: 0 us -> 67 us
  local copies, waits for them, and re-layouts: 63.7 us -> 7.13 us
  starting transfers between devices: 50.2 us -> 0 us
  other arithmetic: 46 us -> 0.66 us
  waiting for transfers between devices: 11.4 us -> 0 us
  matrix products: 9.92 us -> 0 us
    all_gather x1 -> x0, blocking collectives: 67.1 us -> none  [local(): whole = lax.all_gather(near, ('gx', 'gy'))]
    pallas_call x0 -> x3, Pallas kernels: none -> 67 us  [the longest x1 47.9 us: run_fields(): pl.pallas_call(functools.partial(fields_kernel, nx, ny), out_shape=(jax.S...]
    ppermute x16 -> x0, starting transfers between devices: 47.5 us -> none  [passed_along(): lax.ppermute(value, axis, [(source, source + steps) for source in range(f...]
    slice x70 -> x0, local copies, waits for them, and re-layouts: 28.2 us -> none  [the longest x24 12.8 us: ahead(): lax.slice_in_dim(field, 1, count, axis=axis)]
    add x8 -> x0, other arithmetic: 19.5 us -> none  [the longest x4 11.2 us: add(): total + item[1] * (field[:coarse] * field[:coarse] + field[coarse:] * fie...]
    gather x40 -> x0, local copies, waits for them, and re-layouts: 18.4 us -> none
    squeeze x28 -> x0, local copies, waits for them, and re-layouts: 11.3 us -> none  [the longest x14 7.77 us: local(): h = magnetic(e, h, (upper[0], upper[1]), (right[0], right[1]))]
    dot_general x21 -> x0, matrix products: 9.92 us -> none  [the longest x16 3.64 us: add(): field = jnp.dot(first, item[0], preferred_element_type=jnp.float32)]
  transfers between devices with their start and end apart: 17 -> 0, of which waited for: 5 -> 0; matrix products, arithmetic and copies ran while one was open for 19% -> 0% of each run, Pallas kernels for 0% -> 0%
where the time goes in v2:
time: 76.3 us; the launch traced here: 75.5 us
  Pallas kernels  67 us (88%)
  local copies, waits for them, and re-layouts  7.13 us (9%)
    pallas_call x1, Pallas kernels, run_fields(): pl.pallas_call(functools.partial(fields_kernel, nx, ny), out_shape=(jax.S...  47.9 us
    pallas_call x1, Pallas kernels, run_reduce(): pl.pallas_call(functools.partial(reduce_kernel, nx, ny), out_shape=jax.Sh...  11.1 us
    pallas_call x1, Pallas kernels, run_image(): pl.pallas_call(image_kernel, out_shape=jax.ShapeDtypeStruct((IMG, IMG //...  7.94 us
    unnamed x30, local copies, waits for them, and re-layouts  7.13 us

profile of v2, /device:TPU:0, one launch (start us, length us, event | category | flops | bytes accessed | tf_op | source)
XLA Modules:
  0.0 75.5 jit_solution(7267183067563200550)
XLA Ops:
  0.6 0.0 copy-start.12
  0.6 0.7 broadcast_multiply_fusion.factor
  1.3 0.0 copy-done.12
  1.3 0.1 copy.17.shift
  1.4 0.6 copy-done.10
  2.0 0.0 copy-done.11
  2.0 1.1 %copy-done = f32[3,64,8,128]{3,2,1,0:T(8,128)S(1)} copy-done((f32[3,64,8,128]{3,2,1,0:T(8,128)S(1)}, f32[3,64,8,128]{3,2,1,0:T(8,128)}, u32[]{:S(2)}) %copy-start) | copy-done | bytes 786456
  3.1 1.1 %copy-done.1 = f32[3,64,8,128]{3,2,1,0:T(8,128)S(1)} copy-done((f32[3,64,8,128]{3,2,1,0:T(8,128)S(1)}, f32[3,64,8,128]{3,2,1,0:T(8,128)}, u32[]{:S(2)}) %copy-start.1) | copy-done | bytes 786456
  4.3 0.9 %copy-done.5 = s32[64,8,128]{2,1,0:T(8,128)S(1)} copy-done((s32[64,8,128]{2,1,0:T(8,128)S(1)}, s32[64,8,128]{2,1,0:T(8,128)}, u32[]{:S(2)}) %copy-start.5) | copy-done | bytes 262168
  5.2 0.0 copy-start.8
  5.2 47.9 %fields.1 = (f32[3,64,8,128]{3,2,1,0:T(8,128)S(1)}, f32[3,64,8,128]{3,2,1,0:T(8,128)S(1)}, f32[2,128,256]{2,1,0:T(8,128)S(1)}) custom-call(f32[8]{0:T(128)S(1)} %copy-done.10, f32[8]{0:T(128)S(1)} %copy-done.11, f32[3,64,8,128]{3,2,1,0:T(8,128)S(1)} %copy-done, f32[3,64,8,128]{3,2,1,0:T(8,128)S(1)} %copy-done.1, s32[64,8,128]{2,1,0:T(8,128)S(1)} %copy-done.5), custom_call_target="tpu_custom_call" | custom-call | tf_op jit(solution)/shard_map/fields/pallas_call | solution.py:278
  53.1 0.0 copy-done.3
  53.1 0.0 copy-done.4
  53.2 0.0 copy-done.6
  53.2 0.0 copy-done.7
  53.2 0.0 copy-done.8
  53.2 0.0 copy-start.9
  53.2 0.8 %copy-done.9 = s32[128,128]{1,0:T(8,128)S(1)} copy-done((s32[128,128]{1,0:T(8,128)S(1)}, s32[128,128]{1,0:T(8,128)}, u32[]{:S(2)}) %copy-start.9) | copy-done | bytes 65560
  54.0 7.9 %sources.1 = bf16[512,256]{1,0:T(8,128)(2,1)S(1)} custom-call(s32[8,2]{1,0:T(8,128)S(1)} %copy.17.shift, f32[8]{0:T(128)S(1)} %broadcast_multiply_fusion.factor, f32[2,128,256]{2,1,0:T(8,128)S(1)} %get-tuple-element.6.near, f32[256,512]{1,0:T(8,128)S(1)} %copy-done.4, f32[256,256]{1,0:T(8,128)S(1)} %copy-done.8, s32[128,128]{1,0:T(8,128)S(1)} %copy-done.9, ...), custom_call_target="tpu_custom_call" | custom-call | tf_op jit(solution)/shard_map/sources/pallas_call | solution.py:367
  62.0 0.0 copy-done.2
  62.0 11.1 %reduce.1 = f32[16,512]{1,0:T(8,128)S(1)} custom-call(bf16[32,16,256]{2,1,0:T(8,128)(2,1)S(1)} %bitcast.1, f32[256,512]{1,0:T(8,128)S(1)} %copy-done.2), custom_call_target="tpu_custom_call" | custom-call | tf_op jit(solution)/shard_map/reduce/pallas_call | solution.py:411
  73.1 0.6 copy.21
  73.7 0.9 %copy.22 = f32[3,64,8,128]{3,2,1,0:T(8,128)} copy(f32[3,64,8,128]{3,2,1,0:T(8,128)S(1)} %get-tuple-element.13) | data formatting | bytes 1572864
  74.6 0.9 %copy.23 = f32[3,64,8,128]{3,2,1,0:T(8,128)} copy(f32[3,64,8,128]{3,2,1,0:T(8,128)S(1)} %get-tuple-element.14) | data formatting | bytes 1572864
  (10 shorter events, 0.0 us)
Async XLA Ops:
  0.6 0.7 copy-start.12
  1.3 0.7 copy-start.10
  1.3 0.7 copy-start.11
  2.0 1.1 %copy-start = (f32[3,64,8,128]{3,2,1,0:T(8,128)S(1)}, f32[3,64,8,128]{3,2,1,0:T(8,128)}, u32[]{:S(2)}) copy-start(f32[3,64,8,128]{3,2,1,0:T(8,128)} %e_in.1) | copy-start | bytes 2359300
  3.1 1.1 %copy-start.1 = (f32[3,64,8,128]{3,2,1,0:T(8,128)S(1)}, f32[3,64,8,128]{3,2,1,0:T(8,128)}, u32[]{:S(2)}) copy-start(f32[3,64,8,128]{3,2,1,0:T(8,128)} %h_in.1) | copy-start | bytes 2359300
  4.2 0.9 %copy-start.5 = (s32[64,8,128]{2,1,0:T(8,128)S(1)}, s32[64,8,128]{2,1,0:T(8,128)}, u32[]{:S(2)}) copy-start(s32[64,8,128]{2,1,0:T(8,128)} %mat_in.1) | copy-start | bytes 786436
  5.2 47.9 %copy-start.3 = (f32[512,256]{1,0:T(8,128)S(1)}, f32[512,256]{1,0:T(8,128)}, u32[]{:S(2)}) copy-start(f32[512,256]{1,0:T(8,128)} %constant.19.clone.spread) | copy-start | bytes 1572868
  5.2 47.9 %copy-start.4 = (f32[256,512]{1,0:T(8,128)S(1)}, f32[256,512]{1,0:T(8,128)}, u32[]{:S(2)}) copy-start(f32[256,512]{1,0:T(8,128)} %constant.15.clone.table_y) | copy-start | bytes 1572868
  5.2 48.0 %copy-start.6 = (bf16[512,256]{1,0:T(8,128)(2,1)S(1)}, bf16[512,256]{1,0:T(8,128)(2,1)}, u32[]{:S(2)}) copy-start(bf16[512,256]{1,0:T(8,128)(2,1)} %constant.18.clone.first) | copy-start | bytes 786436
  5.2 48.0 %copy-start.7 = (bf16[256,512]{1,0:T(8,128)(2,1)S(1)}, bf16[256,512]{1,0:T(8,128)(2,1)}, u32[]{:S(2)}) copy-start(bf16[256,512]{1,0:T(8,128)(2,1)} %constant.17.clone.second) | copy-start | bytes 786436
  5.2 48.0 %copy-start.8 = (f32[256,256]{1,0:T(8,128)S(1)}, f32[256,256]{1,0:T(8,128)}, u32[]{:S(2)}) copy-start(f32[256,256]{1,0:T(8,128)} %constant.16.clone.table_x) | copy-start | bytes 786436
  53.2 0.8 %copy-start.9 = (s32[128,128]{1,0:T(8,128)S(1)}, s32[128,128]{1,0:T(8,128)}, u32[]{:S(2)}) copy-start(s32[128,128]{1,0:T(8,128)} %mask.1) | copy-start | bytes 196612
  54.0 7.9 %copy-start.2 = (f32[256,512]{1,0:T(8,128)S(1)}, f32[256,512]{1,0:T(8,128)}, u32[]{:S(2)}) copy-start(f32[256,512]{1,0:T(8,128)} %constant.20.clone.spread) | copy-start | bytes 1572868

commit v3 on v2

--- a/solution.py
+++ b/solution.py
@@ -17,7 +17,8 @@
 HIGHEST = lax.Precision.HIGHEST
 VMEM = pl.BlockSpec(memory_space=pltpu.VMEM)
 SMEM = pl.BlockSpec(memory_space=pltpu.SMEM)
-ANY = pl.BlockSpec(memory_space=pl.ANY)
+HBM = pl.BlockSpec(memory_space=pltpu.HBM)
+CHUNK = 8
 
 
 def spectrum_tables(rows_all, cols_all, order):
@@ -83,7 +84,8 @@
         e[c, depth] = zero
         h[c, 0] = zero
     lane = lax.broadcasted_iota(jnp.int32, (rows, cols), 1)
-    row = lax.broadcasted_iota(jnp.int32, (rows, cols), 0)
+    lane3 = lax.broadcasted_iota(jnp.int32, (CHUNK, rows, cols), 2)
+    row3 = lax.broadcasted_iota(jnp.int32, (CHUNK, rows, cols), 1)
     keeps, drives = [], []
     for m in range(perm.shape[0]):
         loss = cond[m] / (2.0 * perm[m])
@@ -125,14 +127,13 @@
         def _():
             x_copy(turn).start()
 
-        def pack(z, face):
-            for k, c in enumerate((first, second)):
+        face = zero
+        for k, c in enumerate((first, second)):
+            for z in range(depth):
                 spot = k * depth + z
-                moved = pltpu.roll(field[c, base + z], lax.rem(spot - edge + cols, cols), 1)
+                moved = pltpu.roll(field[c, base + z], (spot - edge) % cols, 1)
                 face = jnp.where(lane == spot, moved, face)
-            return face
-
-        face_y[turn] = lax.fori_loop(0, depth, pack, zero, unroll=8)
+        face_y[turn] = face
 
         @pl.when(y_to)
         def _():
@@ -148,70 +149,67 @@
         @pl.when(x_from)
         def _():
             x_copy(turn).wait_recv()
+
+    def column(face, first, shift):
+        return jnp.stack([pltpu.roll(face, (shift - first - z) % cols, 1) for z in range(CHUNK)])
 
     def magnetic(turn):
         face = got_y[turn]
         edge_x[...] = got_x[turn].astype(jnp.float32)
-
-        def at(z, carry):
-            ex, ey, ez = e[0, z], e[1, z], e[2, z]
-            ex_z, ey_z = e[0, z + 1], e[1, z + 1]
-            last_row, last_lane = row == rows - 1, lane == cols - 1
-            ey_f = edge_x[0, pl.ds(z, 1), :]
-            ez_f = edge_x[1, pl.ds(z, 1), :]
-            ex_f = pltpu.roll(face, cols - 1 - z, 1)
-            ez_g = pltpu.roll(face, cols - 1 - depth - z, 1)
-            ey_x = jnp.where(last_row, ey_f, pltpu.roll(ey, rows - 1, 0))
-            ez_x = jnp.where(last_row, ez_f, pltpu.roll(ez, rows - 1, 0))
-            ex_y = jnp.where(last_lane, ex_f, pltpu.roll(ex, cols - 1, 1))
-            ez_y = jnp.where(last_lane, ez_g, pltpu.roll(ez, cols - 1, 1))
-            h[0, z + 1] = h[0, z + 1] - COURANT * (ez_y - ez - (ey_z - ey))
-            h[1, z + 1] = h[1, z + 1] - COURANT * (ex_z - ex - (ez_x - ez))
-            h[2, z + 1] = h[2, z + 1] - COURANT * (ey_x - ey - (ex_y - ex))
-            return carry
-
-        lax.fori_loop(0, depth, at, 0, unroll=8)
+        last_row, last_lane = row3 == rows - 1, lane3 == cols - 1
+        for base in range(0, depth, CHUNK):
+            here, next_z = pl.ds(base, CHUNK), pl.ds(base + 1, CHUNK)
+            ex, ey, ez = e[0, here], e[1, here], e[2, here]
+            ex_z, ey_z = e[0, next_z], e[1, next_z]
+            ex_f = column(face, base, cols - 1)
+            ez_f = column(face, depth + base, cols - 1)
+            ey_x = jnp.where(last_row, edge_x[0, here, :][:, None, :], pltpu.roll(ey, rows - 1, 1))
+            ez_x = jnp.where(last_row, edge_x[1, here, :][:, None, :], pltpu.roll(ez, rows - 1, 1))
+            ex_y = jnp.where(last_lane, ex_f, pltpu.roll(ex, cols - 1, 2))
+            ez_y = jnp.where(last_lane, ez_f, pltpu.roll(ez, cols - 1, 2))
+            new_x = h[0, next_z] - COURANT * (ez_y - ez - (ey_z - ey))
+            new_y = h[1, next_z] - COURANT * (ex_z - ex - (ez_x - ez))
+            new_z = h[2, next_z] - COURANT * (ey_x - ey - (ex_y - ex))
+            h[0, next_z] = new_x
+            h[1, next_z] = new_y
+            h[2, next_z] = new_z
 
     def electric(turn):
         face = got_y[turn]
         edge_x[...] = got_x[turn].astype(jnp.float32)
-
-        def at(z, carry):
-            hx, hy, hz = h[0, z + 1], h[1, z + 1], h[2, z + 1]
-            hx_z, hy_z = h[0, z], h[1, z]
-            first_row, first_lane = row == 0, lane == 0
-            hy_f = edge_x[0, pl.ds(z, 1), :]
-            hz_f = edge_x[1, pl.ds(z, 1), :]
-            hx_f = pltpu.roll(face, lax.rem(cols - z, cols), 1)
-            hz_g = pltpu.roll(face, cols - depth - z, 1)
-            hy_x = jnp.where(first_row, hy_f, pltpu.roll(hy, 1, 0))
-            hz_x = jnp.where(first_row, hz_f, pltpu.roll(hz, 1, 0))
-            hx_y = jnp.where(first_lane, hx_f, pltpu.roll(hx, 1, 1))
-            hz_y = jnp.where(first_lane, hz_g, pltpu.roll(hz, 1, 1))
-            kept, driven = keep[z], drive[z]
-            e[0, z] = kept * e[0, z] + driven * (hz - hz_y - (hy - hy_z))
-            e[1, z] = kept * e[1, z] + driven * (hx - hx_z - (hz - hz_x))
-            e[2, z] = kept * e[2, z] + driven * (hy - hy_x - (hx - hx_y))
-            return carry
-
-        lax.fori_loop(0, depth, at, 0, unroll=8)
+        first_row, first_lane = row3 == 0, lane3 == 0
+        for base in range(0, depth, CHUNK):
+            here, next_z = pl.ds(base, CHUNK), pl.ds(base + 1, CHUNK)
+            hx, hy, hz = h[0, next_z], h[1, next_z], h[2, next_z]
+            hx_z, hy_z = h[0, here], h[1, here]
+            hx_f = column(face, base, 0)
+            hz_f = column(face, depth + base, 0)
+            hy_x = jnp.where(first_row, edge_x[0, here, :][:, None, :], pltpu.roll(hy, 1, 1))
+            hz_x = jnp.where(first_row, edge_x[1, here, :][:, None, :], pltpu.roll(hz, 1, 1))
+            hx_y = jnp.where(first_lane, hx_f, pltpu.roll(hx, 1, 2))
+            hz_y = jnp.where(first_lane, hz_f, pltpu.roll(hz, 1, 2))
+            kept, driven = keep[here], drive[here]
+            new_x = kept * e[0, here] + driven * (hz - hz_y - (hy - hy_z))
+            new_y = kept * e[1, here] + driven * (hx - hx_z - (hz - hz_x))
+            new_z = kept * e[2, here] + driven * (hy - hy_x - (hx - hx_y))
+            e[0, here] = new_x
+            e[1, here] = new_y
+            e[2, here] = new_z
 
     loads[0].wait()
     start(0)
     loads[2].wait()
 
-    def look_up(z, carry):
-        index = mat[z]
-        kept, driven = zero, zero
+    for base in range(0, depth, CHUNK):
+        index = mat[base:base + CHUNK]
+        kept, driven = jnp.zeros_like(index, jnp.float32), jnp.zeros_like(index, jnp.float32)
         for m in range(len(keeps)):
             chosen = index == m
             kept = jnp.where(chosen, keeps[m], kept)
             driven = jnp.where(chosen, drives[m], driven)
-        keep[z] = kept
-        drive[z] = driven
-        return carry
-
-    lax.fori_loop(0, depth, look_up, 0, unroll=4)
+        keep[base:base + CHUNK] = kept
+        drive[base:base + CHUNK] = driven
+
     loads[1].wait()
     for turn in range(2 * STEPS):
         if turn:
@@ -282,8 +280,8 @@
             jax.ShapeDtypeStruct(h_field.shape, f32),
             jax.ShapeDtypeStruct((2, rows * nx, cols * ny), f32),
         ),
-        in_specs=[SMEM, SMEM, ANY, ANY, ANY],
-        out_specs=(ANY, ANY, VMEM),
+        in_specs=[SMEM, SMEM, HBM, HBM, HBM],
+        out_specs=(HBM, HBM, VMEM),
         scratch_shapes=[
             pltpu.VMEM((3, depth + 1, rows, cols), f32),
             pltpu.VMEM((3, depth + 1, rows, cols), f32),
@@ -299,15 +297,22 @@
             dma((devices,)), dma((devices,)),
         ],
         compiler_params=pltpu.CompilerParams(
-            collective_id=0, has_side_effects=True, vmem_limit_bytes=40 * 2**20
+            collective_id=0, has_side_effects=True, vmem_limit_bytes=61 * 2**20
         ),
         name="fields",
     )(permittivity, conductivity, e_field, h_field, material)
 
 
 def image_kernel(
-    shift, factor, near, table_y, table_x, mask, second, first, spread, tall, spec, total
+    sources, shift, weight, e_in, h_in, near, table_y, table_x, mask, second, first, spread, tall, e_out, h_out, spec, total,
+    sem,
 ):
+    moves = (
+        pltpu.make_async_copy(e_in, e_out, sem.at[0]),
+        pltpu.make_async_copy(h_in, h_out, sem.at[1]),
+    )
+    for move in moves:
+        move.start()
     pols, order = near.shape[0], table_x.shape[0]
     window, coarse = mask.shape[0], spread.shape[1]
     for p in range(pols):
@@ -351,32 +356,39 @@
         power = field * field
         power = power[:coarse] + power[coarse:]
         power = sum(power[:, p * coarse:(p + 1) * coarse] for p in range(pols))
-        total[...] += factor[s] * power
+        total[...] += weight[s] * (1.0 / sources) * power
         return carry
 
     lax.fori_loop(0, shift.shape[0], add, 0)
     tall[...] = jnp.dot(
         spread[...], total[...], precision=HIGHEST, preferred_element_type=jnp.float32
     ).astype(jnp.bfloat16).reshape(tall.shape)
-
-
-def run_image(src_shift, factors, near, pupil_mask, devices):
+    for move in moves:
+        move.wait()
+
+
+def run_image(src_shift, src_weight, e, h, near, pupil_mask, devices):
     rows_all, cols_all = near.shape[1], near.shape[2]
     table_y, table_x = spectrum_tables(rows_all, cols_all, K)
     second, first, spread = image_tables(PW, IMG)
-    tall = pl.pallas_call(
-        image_kernel,
-        out_shape=jax.ShapeDtypeStruct((IMG, IMG // 2), jnp.bfloat16),
-        in_specs=[SMEM, SMEM] + [VMEM] * 7,
-        out_specs=VMEM,
+    tall, e, h = pl.pallas_call(
+        functools.partial(image_kernel, src_shift.shape[0] * devices),
+        out_shape=(
+            jax.ShapeDtypeStruct((IMG, IMG // 2), jnp.bfloat16),
+            jax.ShapeDtypeStruct(e.shape, e.dtype),
+            jax.ShapeDtypeStruct(h.shape, h.dtype),
+        ),
+        in_specs=[SMEM, SMEM, HBM, HBM] + [VMEM] * 7,
+        out_specs=(VMEM, HBM, HBM),
         scratch_shapes=[
             pltpu.VMEM((2, 2 * K // PW, K, PW), jnp.float32),
             pltpu.VMEM((IMG // 2, IMG // 2), jnp.float32),
+            pltpu.SemaphoreType.DMA((2,)),
         ],
-        compiler_params=pltpu.CompilerParams(vmem_limit_bytes=40 * 2**20),
+        compiler_params=pltpu.CompilerParams(vmem_limit_bytes=60 * 2**20),
         name="sources",
-    )(src_shift, factors, near, table_y, table_x, pupil_mask, second, first, spread)
-    return tall.reshape(devices, IMG // devices, IMG // 2), spread
+    )(src_shift, src_weight, e, h, near, table_y, table_x, pupil_mask, second, first, spread)
+    return tall.reshape(devices, IMG // devices, IMG // 2), spread, e, h
 
 
 def reduce_kernel(nx, ny, tall, spread, image, got, send, recv):
@@ -431,8 +443,7 @@
     nx, ny = lax.axis_size("gx"), lax.axis_size("gy")
     devices = nx * ny
     e, h, near = run_fields(e_field, h_field, material, permittivity, conductivity, nx, ny)
-    factors = src_weight / (src_shift.shape[0] * devices)
-    tall, spread = run_image(src_shift, factors, near, pupil_mask, devices)
+    tall, spread, e, h = run_image(src_shift, src_weight, e, h, near, pupil_mask, devices)
     image = run_reduce(tall, spread, nx, ny)
     return (image, e, h)
 

time: 76.3 us -> 107 us (1.40)
  Pallas kernels: 67 us -> 104 us
  local copies, waits for them, and re-layouts: 7.13 us -> 2.91 us
    pallas_call x1, Pallas kernels: 7.94 us -> 51.1 us  [run_image(): pl.pallas_call(functools.partial(image_kernel, src_shift.shape[0] * devic...]
    pallas_call x1, Pallas kernels: 47.9 us -> 40.3 us  [run_fields(): pl.pallas_call(functools.partial(fields_kernel, nx, ny), out_shape=(jax.S...]
    unnamed x30 -> x6, local copies, waits for them, and re-layouts: 7.13 us -> 2.91 us
    pallas_call x1, Pallas kernels: 11.1 us -> 12.2 us  [run_reduce(): pl.pallas_call(functools.partial(reduce_kernel, nx, ny), out_shape=jax.Sh...]
where the time goes in v3:
time: 107 us
  Pallas kernels  104 us (97%)
  local copies, waits for them, and re-layouts  2.91 us (3%)
    pallas_call x1, Pallas kernels, run_image(): pl.pallas_call(functools.partial(image_kernel, src_shift.shape[0] * devic...  51.1 us
    pallas_call x1, Pallas kernels, run_fields(): pl.pallas_call(functools.partial(fields_kernel, nx, ny), out_shape=(jax.S...  40.3 us
    pallas_call x1, Pallas kernels, run_reduce(): pl.pallas_call(functools.partial(reduce_kernel, nx, ny), out_shape=jax.Sh...  12.2 us
    unnamed x6, local copies, waits for them, and re-layouts  2.91 us

profile of v3, /device:TPU:0, one launch (start us, length us, event | category | flops | bytes accessed | tf_op | source)
XLA Modules:
  0.0 107.2 jit_solution(7226884727842045671)
XLA Ops:
  0.6 1.3 %copy.17.shift = s32[8,2]{1,0:T(8,128)} copy(s32[8,2]{0,1:T(2,128)} %param.19) | data formatting | bytes 128 | tf_op args[5]
  2.0 40.3 %fields.1 = (f32[3,64,8,128]{3,2,1,0:T(8,128)}, f32[3,64,8,128]{3,2,1,0:T(8,128)}, f32[2,128,256]{2,1,0:T(8,128)}) custom-call(f32[8]{0:T(128)} %perm.1, f32[8]{0:T(128)} %cond.1, f32[3,64,8,128]{3,2,1,0:T(8,128)} %e_in.1, f32[3,64,8,128]{3,2,1,0:T(8,128)} %h_in.1, s32[64,8,128]{2,1,0:T(8,128)} %mat_in.1), custom_call_target="tpu_custom_call" | custom-call | tf_op jit(solution)/shard_map/fields/pallas_call | solution.py:276
  42.3 0.0 copy-start
  42.3 51.1 %sources.1 = (bf16[512,256]{1,0:T(8,128)(2,1)}, f32[3,64,8,128]{3,2,1,0:T(8,128)}, f32[3,64,8,128]{3,2,1,0:T(8,128)}) custom-call(s32[8,2]{1,0:T(8,128)} %copy.17.shift, f32[8]{0:T(128)} %weight.1, f32[3,64,8,128]{3,2,1,0:T(8,128)} %get-tuple-element.9.e_in, f32[3,64,8,128]{3,2,1,0:T(8,128)} %get-tuple-element.10.h_in, ...), custom_call_target="tpu_custom_call" | custom-call | tf_op jit(solution)/shard_map/sources/pallas_call | solution.py:374
  93.3 0.0 copy-done
  93.4 0.0 copy-start.1
  93.4 0.9 copy-done.1
  94.3 12.2 %reduce.1 = f32[16,512]{1,0:T(8,128)S(1)} custom-call(bf16[32,16,256]{2,1,0:T(8,128)(2,1)S(1)} %bitcast.1, f32[256,512]{1,0:T(8,128)S(1)} %copy-done), custom_call_target="tpu_custom_call" | custom-call | tf_op jit(solution)/shard_map/reduce/pallas_call | solution.py:423
  106.5 0.6 copy.19
Async XLA Ops:
  42.3 51.1 %copy-start = (f32[256,512]{1,0:T(8,128)S(1)}, f32[256,512]{1,0:T(8,128)}, u32[]{:S(2)}) copy-start(f32[256,512]{1,0:T(8,128)} %constant.17.clone.spread) | copy-start | bytes 1572868
  93.4 1.0 copy-start.1

commit v4 on v3

--- a/solution.py
+++ b/solution.py
@@ -19,6 +19,7 @@
 SMEM = pl.BlockSpec(memory_space=pltpu.SMEM)
 HBM = pl.BlockSpec(memory_space=pltpu.HBM)
 CHUNK = 8
+FIELDS_MIB = 60
 
 
 def spectrum_tables(rows_all, cols_all, order):
@@ -61,8 +62,8 @@
 
 
 def fields_kernel(
-    nx, ny, perm, cond, e_in, h_in, mat_in, e_out, h_out, near,
-    e, h, mat, keep, drive, edge_x, face_x, face_y, got_x, got_y, in_sem, x_send, x_recv, y_send, y_recv,
+    nx, ny, perm, cond, e_in, h_in, mat_in, e, h, near,
+    mat, keep, drive, edge_x, face_x, face_y, got_x, got_y, in_sem, x_send, x_recv, y_send, y_recv,
     n_send, n_recv,
 ):
     depth = mat.shape[0]
@@ -70,8 +71,8 @@
     gx, gy = lax.axis_index("gx"), lax.axis_index("gy")
     me = gx * ny + gy
     loads = (
-        pltpu.make_async_copy(e_in, e.at[:, pl.ds(0, depth)], in_sem.at[0]),
-        pltpu.make_async_copy(h_in, h.at[:, pl.ds(1, depth)], in_sem.at[1]),
+        pltpu.make_async_copy(e_in, e, in_sem.at[0]),
+        pltpu.make_async_copy(h_in, h, in_sem.at[1]),
         pltpu.make_async_copy(mat_in, mat, in_sem.at[2]),
     )
     for load in loads:
@@ -80,9 +81,6 @@
     got_y[...] = jnp.zeros_like(got_y)
     greet_all(nx, ny, me)
     zero = jnp.zeros((rows, cols), jnp.float32)
-    for c in range(3):
-        e[c, depth] = zero
-        h[c, 0] = zero
     lane = lax.broadcasted_iota(jnp.int32, (rows, cols), 1)
     lane3 = lax.broadcasted_iota(jnp.int32, (CHUNK, rows, cols), 2)
     row3 = lax.broadcasted_iota(jnp.int32, (CHUNK, rows, cols), 1)
@@ -117,11 +115,11 @@
         return gx > 0, gy > 0
 
     def start(turn):
-        field, base, edge, first, second = (e, 0, 0, 0, 2) if turn % 2 == 0 else (h, 1, cols - 1, 0, 2)
+        field, edge, first, second = (e, 0, 0, 2) if turn % 2 == 0 else (h, cols - 1, 0, 2)
         at_row = 0 if turn % 2 == 0 else rows - 1
         x_to, y_to = sends(turn)
         for k, c in enumerate((1, 2)):
-            face_x[turn, k] = field[c, pl.ds(base, depth), at_row, :].astype(jnp.bfloat16)
+            face_x[turn, k] = field[c, :, at_row, :].astype(jnp.bfloat16)
 
         @pl.when(x_to)
         def _():
@@ -131,7 +129,7 @@
         for k, c in enumerate((first, second)):
             for z in range(depth):
                 spot = k * depth + z
-                moved = pltpu.roll(field[c, base + z], (spot - edge) % cols, 1)
+                moved = pltpu.roll(field[c, z], (spot - edge) % cols, 1)
                 face = jnp.where(lane == spot, moved, face)
         face_y[turn] = face
 
@@ -152,36 +150,48 @@
 
     def column(face, first, shift):
         return jnp.stack([pltpu.roll(face, (shift - first - z) % cols, 1) for z in range(CHUNK)])
+
+    def above(field, c, base):
+        end = min(base + 1 + CHUNK, depth)
+        value = field[c, base + 1:end]
+        if end == depth:
+            value = jnp.concatenate((value, zero[None]), axis=0)
+        return value
+
+    def below(field, c, base):
+        if base:
+            return field[c, base - 1:base - 1 + CHUNK]
+        return jnp.concatenate((zero[None], field[c, :CHUNK - 1]), axis=0)
 
     def magnetic(turn):
         face = got_y[turn]
         edge_x[...] = got_x[turn].astype(jnp.float32)
         last_row, last_lane = row3 == rows - 1, lane3 == cols - 1
         for base in range(0, depth, CHUNK):
-            here, next_z = pl.ds(base, CHUNK), pl.ds(base + 1, CHUNK)
+            here = pl.ds(base, CHUNK)
             ex, ey, ez = e[0, here], e[1, here], e[2, here]
-            ex_z, ey_z = e[0, next_z], e[1, next_z]
+            ex_z, ey_z = above(e, 0, base), above(e, 1, base)
             ex_f = column(face, base, cols - 1)
             ez_f = column(face, depth + base, cols - 1)
             ey_x = jnp.where(last_row, edge_x[0, here, :][:, None, :], pltpu.roll(ey, rows - 1, 1))
             ez_x = jnp.where(last_row, edge_x[1, here, :][:, None, :], pltpu.roll(ez, rows - 1, 1))
             ex_y = jnp.where(last_lane, ex_f, pltpu.roll(ex, cols - 1, 2))
             ez_y = jnp.where(last_lane, ez_f, pltpu.roll(ez, cols - 1, 2))
-            new_x = h[0, next_z] - COURANT * (ez_y - ez - (ey_z - ey))
-            new_y = h[1, next_z] - COURANT * (ex_z - ex - (ez_x - ez))
-            new_z = h[2, next_z] - COURANT * (ey_x - ey - (ex_y - ex))
-            h[0, next_z] = new_x
-            h[1, next_z] = new_y
-            h[2, next_z] = new_z
+            new_x = h[0, here] - COURANT * (ez_y - ez - (ey_z - ey))
+            new_y = h[1, here] - COURANT * (ex_z - ex - (ez_x - ez))
+            new_z = h[2, here] - COURANT * (ey_x - ey - (ex_y - ex))
+            h[0, here] = new_x
+            h[1, here] = new_y
+            h[2, here] = new_z
 
     def electric(turn):
         face = got_y[turn]
         edge_x[...] = got_x[turn].astype(jnp.float32)
         first_row, first_lane = row3 == 0, lane3 == 0
         for base in range(0, depth, CHUNK):
-            here, next_z = pl.ds(base, CHUNK), pl.ds(base + 1, CHUNK)
-            hx, hy, hz = h[0, next_z], h[1, next_z], h[2, next_z]
-            hx_z, hy_z = h[0, here], h[1, here]
+            here = pl.ds(base, CHUNK)
+            hx, hy, hz = h[0, here], h[1, here], h[2, here]
+            hx_z, hy_z = below(h, 0, base), below(h, 1, base)
             hx_f = column(face, base, 0)
             hz_f = column(face, depth + base, 0)
             hy_x = jnp.where(first_row, edge_x[0, here, :][:, None, :], pltpu.roll(hy, 1, 1))
@@ -220,11 +230,6 @@
         else:
             electric(turn)
 
-    store_h = pltpu.make_async_copy(h.at[:, pl.ds(1, depth)], h_out, in_sem.at[1])
-    store_e = pltpu.make_async_copy(e.at[:, pl.ds(0, depth)], e_out, in_sem.at[0])
-    store_h.start()
-    store_e.start()
-
     def spot(index):
         x_at = pl.multiple_of((index // ny) * rows, rows)
         y_at = pl.multiple_of(lax.rem(index, ny) * cols, cols)
@@ -264,9 +269,6 @@
         @pl.when(y_to)
         def _():
             y_copy(turn).wait_send()
-
-    store_h.wait()
-    store_e.wait()
 
 
 def run_fields(e_field, h_field, material, permittivity, conductivity, nx, ny):
@@ -281,10 +283,8 @@
             jax.ShapeDtypeStruct((2, rows * nx, cols * ny), f32),
         ),
         in_specs=[SMEM, SMEM, HBM, HBM, HBM],
-        out_specs=(HBM, HBM, VMEM),
+        out_specs=(VMEM, VMEM, VMEM),
         scratch_shapes=[
-            pltpu.VMEM((3, depth + 1, rows, cols), f32),
-            pltpu.VMEM((3, depth + 1, rows, cols), f32),
             pltpu.VMEM((depth, rows, cols), jnp.int32),
             pltpu.VMEM((depth, rows, cols), f32),
             pltpu.VMEM((depth, rows, cols), f32),
@@ -297,22 +297,15 @@
             dma((devices,)), dma((devices,)),
         ],
         compiler_params=pltpu.CompilerParams(
-            collective_id=0, has_side_effects=True, vmem_limit_bytes=61 * 2**20
+            collective_id=0, has_side_effects=True, vmem_limit_bytes=FIELDS_MIB * 2**20
         ),
         name="fields",
     )(permittivity, conductivity, e_field, h_field, material)
 
 
 def image_kernel(
-    sources, shift, weight, e_in, h_in, near, table_y, table_x, mask, second, first, spread, tall, e_out, h_out, spec, total,
-    sem,
+    sources, shift, weight, near, table_y, table_x, mask, second, first, spread, tall, spec, total,
 ):
-    moves = (
-        pltpu.make_async_copy(e_in, e_out, sem.at[0]),
-        pltpu.make_async_copy(h_in, h_out, sem.at[1]),
-    )
-    for move in moves:
-        move.start()
     pols, order = near.shape[0], table_x.shape[0]
     window, coarse = mask.shape[0], spread.shape[1]
     for p in range(pols):
@@ -363,32 +356,25 @@
     tall[...] = jnp.dot(
         spread[...], total[...], precision=HIGHEST, preferred_element_type=jnp.float32
     ).astype(jnp.bfloat16).reshape(tall.shape)
-    for move in moves:
-        move.wait()
-
-
-def run_image(src_shift, src_weight, e, h, near, pupil_mask, devices):
+
+
+def run_image(src_shift, src_weight, near, pupil_mask, devices):
     rows_all, cols_all = near.shape[1], near.shape[2]
     table_y, table_x = spectrum_tables(rows_all, cols_all, K)
     second, first, spread = image_tables(PW, IMG)
-    tall, e, h = pl.pallas_call(
+    tall = pl.pallas_call(
         functools.partial(image_kernel, src_shift.shape[0] * devices),
-        out_shape=(
-            jax.ShapeDtypeStruct((IMG, IMG // 2), jnp.bfloat16),
-            jax.ShapeDtypeStruct(e.shape, e.dtype),
-            jax.ShapeDtypeStruct(h.shape, h.dtype),
-        ),
-        in_specs=[SMEM, SMEM, HBM, HBM] + [VMEM] * 7,
-        out_specs=(VMEM, HBM, HBM),
+        out_shape=jax.ShapeDtypeStruct((IMG, IMG // 2), jnp.bfloat16),
+        in_specs=[SMEM, SMEM] + [VMEM] * 7,
+        out_specs=VMEM,
         scratch_shapes=[
             pltpu.VMEM((2, 2 * K // PW, K, PW), jnp.float32),
             pltpu.VMEM((IMG // 2, IMG // 2), jnp.float32),
-            pltpu.SemaphoreType.DMA((2,)),
         ],
-        compiler_params=pltpu.CompilerParams(vmem_limit_bytes=60 * 2**20),
+        compiler_params=pltpu.CompilerParams(vmem_limit_bytes=40 * 2**20),
         name="sources",
-    )(src_shift, src_weight, e, h, near, table_y, table_x, pupil_mask, second, first, spread)
-    return tall.reshape(devices, IMG // devices, IMG // 2), spread, e, h
+    )(src_shift, src_weight, near, table_y, table_x, pupil_mask, second, first, spread)
+    return tall.reshape(devices, IMG // devices, IMG // 2), spread
 
 
 def reduce_kernel(nx, ny, tall, spread, image, got, send, recv):
@@ -443,7 +429,7 @@
     nx, ny = lax.axis_size("gx"), lax.axis_size("gy")
     devices = nx * ny
     e, h, near = run_fields(e_field, h_field, material, permittivity, conductivity, nx, ny)
-    tall, spread, e, h = run_image(src_shift, src_weight, e, h, near, pupil_mask, devices)
+    tall, spread = run_image(src_shift, src_weight, near, pupil_mask, devices)
     image = run_reduce(tall, spread, nx, ny)
     return (image, e, h)
 

time: 107 us -> 68.6 us (0.64)
  Pallas kernels: 104 us -> 61.4 us
  local copies, waits for them, and re-layouts: 2.91 us -> 6.09 us
    pallas_call x1, Pallas kernels: 51.1 us -> 7.92 us  [run_image(): pl.pallas_call(functools.partial(image_kernel, src_shift.shape[0] * devic...]
    unnamed x6 -> x26, local copies, waits for them, and re-layouts: 2.91 us -> 6.09 us
where the time goes in v4:
time: 68.6 us; the launch traced here: 68.3 us
  Pallas kernels  61.4 us (90%)
  local copies, waits for them, and re-layouts  6.09 us (9%)
  between operations  0.73 us (1%)
    pallas_call x1, Pallas kernels, run_fields(): pl.pallas_call(functools.partial(fields_kernel, nx, ny), out_shape=(jax.S...  41 us
    pallas_call x1, Pallas kernels, run_reduce(): pl.pallas_call(functools.partial(reduce_kernel, nx, ny), out_shape=jax.Sh...  12.6 us
    pallas_call x1, Pallas kernels, run_image(): pl.pallas_call(functools.partial(image_kernel, src_shift.shape[0] * devic...  7.92 us
    unnamed x26, local copies, waits for them, and re-layouts  6.09 us

profile of v4, /device:TPU:0, one launch (start us, length us, event | category | flops | bytes accessed | tf_op | source)
XLA Modules:
  0.0 68.3 jit_solution(9919732844263102165)
XLA Ops:
  0.6 0.8 %copy.17.shift = s32[8,2]{1,0:T(8,128)S(1)} copy(s32[8,2]{0,1:T(2,128)} %param.19) | data formatting | bytes 128 | tf_op args[5]
  1.4 0.0 copy-start.1
  1.4 0.0 copy-start.2
  1.4 0.0 copy-start.3
  1.4 0.0 copy-start.5
  1.4 41.0 %fields.1 = (f32[3,64,8,128]{3,2,1,0:T(8,128)}, f32[3,64,8,128]{3,2,1,0:T(8,128)}, f32[2,128,256]{2,1,0:T(8,128)}) custom-call(f32[8]{0:T(128)} %perm.1, f32[8]{0:T(128)} %cond.1, f32[3,64,8,128]{3,2,1,0:T(8,128)} %e_in.1, f32[3,64,8,128]{3,2,1,0:T(8,128)} %h_in.1, s32[64,8,128]{2,1,0:T(8,128)} %mat_in.1), custom_call_target="tpu_custom_call" | custom-call | tf_op jit(solution)/shard_map/fields/pallas_call | solution.py:278
  42.4 0.0 copy-start.8
  42.4 0.0 copy-done.1
  42.4 0.0 copy-done.2
  42.4 0.0 copy-done.3
  42.4 0.0 copy-done.4
  42.4 0.0 copy-done.5
  42.4 0.6 copy-done.8
  43.0 0.9 %copy-done.6 = f32[2,128,256]{2,1,0:T(8,128)S(1)} copy-done((f32[2,128,256]{2,1,0:T(8,128)S(1)}, f32[2,128,256]{2,1,0:T(8,128)}, u32[]{:S(2)}) %copy-start.6) | copy-done | bytes 262168
  44.0 0.8 %copy-done.7 = s32[128,128]{1,0:T(8,128)S(1)} copy-done((s32[128,128]{1,0:T(8,128)S(1)}, s32[128,128]{1,0:T(8,128)}, u32[]{:S(2)}) %copy-start.7) | copy-done | bytes 65560
  44.8 7.9 %sources.1 = bf16[512,256]{1,0:T(8,128)(2,1)S(1)} custom-call(s32[8,2]{1,0:T(8,128)S(1)} %copy.17.shift, f32[8]{0:T(128)S(1)} %copy-done.8, f32[2,128,256]{2,1,0:T(8,128)S(1)} %copy-done.6, f32[256,512]{1,0:T(8,128)S(1)} %copy-done.2, f32[256,256]{1,0:T(8,128)S(1)} %copy-done.5, s32[128,128]{1,0:T(8,128)S(1)} %copy-done.7, bf16[256,512]{1,0:T(8,128)(2,1)S(1)} %copy-done.4, ...), custom_call_target="tpu_custom_call" | custom-call | tf_op jit(solution)/shard_map/sources/pallas_call | solution.py:365
  52.8 0.0 copy-start.10
  52.8 0.0 copy-done
  52.8 12.6 %reduce.1 = f32[16,512]{1,0:T(8,128)S(1)} custom-call(bf16[32,16,256]{2,1,0:T(8,128)(2,1)S(1)} %bitcast.1, f32[256,512]{1,0:T(8,128)S(1)} %copy-done), custom_call_target="tpu_custom_call" | custom-call | tf_op jit(solution)/shard_map/reduce/pallas_call | solution.py:409
  65.3 0.6 copy.21
  66.0 0.0 copy-done.10
  66.0 0.9 %copy.22 = f32[3,64,8,128]{3,2,1,0:T(8,128)} copy(f32[3,64,8,128]{3,2,1,0:T(8,128)S(1)} %copy-done.10) | data formatting | bytes 1572864
  66.8 0.5 copy-done.9
  67.4 0.9 %copy.23 = f32[3,64,8,128]{3,2,1,0:T(8,128)} copy(f32[3,64,8,128]{3,2,1,0:T(8,128)S(1)} %copy-done.9) | data formatting | bytes 1572864
  (5 shorter events, 0.0 us)
Async XLA Ops:
  1.4 41.0 %copy-start.1 = (f32[512,256]{1,0:T(8,128)S(1)}, f32[512,256]{1,0:T(8,128)}, u32[]{:S(2)}) copy-start(f32[512,256]{1,0:T(8,128)} %constant.16.clone.spread) | copy-start | bytes 1572868
  1.4 41.0 %copy-start.2 = (f32[256,512]{1,0:T(8,128)S(1)}, f32[256,512]{1,0:T(8,128)}, u32[]{:S(2)}) copy-start(f32[256,512]{1,0:T(8,128)} %constant.12.clone.table_y) | copy-start | bytes 1572868
  1.4 41.0 %copy-start.3 = (bf16[512,256]{1,0:T(8,128)(2,1)S(1)}, bf16[512,256]{1,0:T(8,128)(2,1)}, u32[]{:S(2)}) copy-start(bf16[512,256]{1,0:T(8,128)(2,1)} %constant.15.clone.first) | copy-start | bytes 786436
  1.4 41.0 %copy-start.4 = (bf16[256,512]{1,0:T(8,128)(2,1)S(1)}, bf16[256,512]{1,0:T(8,128)(2,1)}, u32[]{:S(2)}) copy-start(bf16[256,512]{1,0:T(8,128)(2,1)} %constant.14.clone.second) | copy-start | bytes 786436
  1.4 41.0 %copy-start.5 = (f32[256,256]{1,0:T(8,128)S(1)}, f32[256,256]{1,0:T(8,128)}, u32[]{:S(2)}) copy-start(f32[256,256]{1,0:T(8,128)} %constant.13.clone.table_x) | copy-start | bytes 786436
  42.4 0.7 copy-start.8
  43.0 0.9 %copy-start.6 = (f32[2,128,256]{2,1,0:T(8,128)S(1)}, f32[2,128,256]{2,1,0:T(8,128)}, u32[]{:S(2)}) copy-start(f32[2,128,256]{2,1,0:T(8,128)} %get-tuple-element.6.near) | copy-start | bytes 786436
  44.0 0.8 %copy-start.7 = (s32[128,128]{1,0:T(8,128)S(1)}, s32[128,128]{1,0:T(8,128)}, u32[]{:S(2)}) copy-start(s32[128,128]{1,0:T(8,128)} %mask.1) | copy-start | bytes 196612
  44.8 7.9 %copy-start = (f32[256,512]{1,0:T(8,128)S(1)}, f32[256,512]{1,0:T(8,128)}, u32[]{:S(2)}) copy-start(f32[256,512]{1,0:T(8,128)} %constant.17.clone.spread) | copy-start | bytes 1572868
  52.8 13.2 %copy-start.10 = (f32[3,64,8,128]{3,2,1,0:T(8,128)S(1)}, f32[3,64,8,128]{3,2,1,0:T(8,128)}, u32[]{:S(2)}) copy-start(f32[3,64,8,128]{3,2,1,0:T(8,128)} %get-tuple-element.13) | copy-start | bytes 2359300
  66.0 1.4 %copy-start.9 = (f32[3,64,8,128]{3,2,1,0:T(8,128)S(1)}, f32[3,64,8,128]{3,2,1,0:T(8,128)}, u32[]{:S(2)}) copy-start(f32[3,64,8,128]{3,2,1,0:T(8,128)} %get-tuple-element.14) | copy-start | bytes 2359300

commit v5 on v4

--- a/solution.py
+++ b/solution.py
@@ -63,8 +63,8 @@
 
 def fields_kernel(
     nx, ny, perm, cond, e_in, h_in, mat_in, e, h, near,
-    mat, keep, drive, edge_x, face_x, face_y, got_x, got_y, in_sem, x_send, x_recv, y_send, y_recv,
-    n_send, n_recv,
+    mat, keep, drive, own, edge_x, up_out, low_out, pack_out, up_in, low_in, pack_in, far_row, far_col,
+    in_sem, f_send, f_recv, n_send, n_recv,
 ):
     depth = mat.shape[0]
     rows, cols = mat.shape[1], mat.shape[2]
@@ -77,8 +77,8 @@
     )
     for load in loads:
         load.start()
-    got_x[...] = jnp.zeros_like(got_x)
-    got_y[...] = jnp.zeros_like(got_y)
+    for landing in (up_in, low_in, pack_in, far_row, far_col):
+        landing[...] = jnp.zeros_like(landing)
     greet_all(nx, ny, me)
     zero = jnp.zeros((rows, cols), jnp.float32)
     lane = lax.broadcasted_iota(jnp.int32, (rows, cols), 1)
@@ -90,63 +90,99 @@
         keeps.append((1.0 - loss) / (1.0 + loss))
         drives.append(COURANT / (perm[m] * (1.0 + loss)))
 
-    def x_copy(turn):
-        to = gx - 1 if turn % 2 == 0 else gx + 1
-        return pltpu.make_async_remote_copy(
-            src_ref=face_x.at[turn], dst_ref=got_x.at[turn], send_sem=x_send.at[turn],
-            recv_sem=x_recv.at[turn], device_id=(to, gy), device_id_type=MESH,
-        )
-
-    def y_copy(turn):
-        to = gy - 1 if turn % 2 == 0 else gy + 1
-        return pltpu.make_async_remote_copy(
-            src_ref=face_y.at[turn], dst_ref=got_y.at[turn], send_sem=y_send.at[turn],
-            recv_sem=y_recv.at[turn], device_id=(gx, to), device_id_type=MESH,
-        )
-
-    def sends(turn):
-        if turn % 2 == 0:
-            return gx > 0, gy > 0
-        return gx < nx - 1, gy < ny - 1
-
-    def gets(turn):
-        if turn % 2 == 0:
-            return gx < nx - 1, gy < ny - 1
-        return gx > 0, gy > 0
-
-    def start(turn):
-        field, edge, first, second = (e, 0, 0, 2) if turn % 2 == 0 else (h, cols - 1, 0, 2)
-        at_row = 0 if turn % 2 == 0 else rows - 1
-        x_to, y_to = sends(turn)
-        for k, c in enumerate((1, 2)):
-            face_x[turn, k] = field[c, :, at_row, :].astype(jnp.bfloat16)
-
-        @pl.when(x_to)
-        def _():
-            x_copy(turn).start()
-
+    west, east = gx > 0, gx < nx - 1
+    south, north = gy > 0, gy < ny - 1
+
+    def copies(step):
+        routes = (
+            (east, west, low_out.at[step], low_in.at[step], 1, 0),
+            (west, east, up_out.at[step], up_in.at[step], -1, 0),
+            (south, north, pack_out.at[step, 0], pack_in.at[step, 0], 0, -1),
+            (north, south, pack_out.at[step, pl.ds(1, 3)], pack_in.at[step, pl.ds(1, 3)], 0, 1),
+            (
+                jnp.logical_and(east, south), jnp.logical_and(west, north),
+                low_out.at[step, 0], far_row.at[step], 1, -1,
+            ),
+            (
+                jnp.logical_and(west, north), jnp.logical_and(east, south),
+                pack_out.at[step, 3], far_col.at[step], -1, 1,
+            ),
+        )
+        return [
+            (
+                sends, gets,
+                pltpu.make_async_remote_copy(
+                    src_ref=src, dst_ref=dst, send_sem=f_send.at[step, kind],
+                    recv_sem=f_recv.at[step, kind], device_id=(gx + dx, gy + dy),
+                    device_id_type=MESH,
+                ),
+            )
+            for kind, (sends, gets, src, dst, dx, dy) in enumerate(routes)
+        ]
+
+    def packed(parts, edge):
         face = zero
-        for k, c in enumerate((first, second)):
+        for k, (field, c) in enumerate(parts):
             for z in range(depth):
                 spot = k * depth + z
                 moved = pltpu.roll(field[c, z], (spot - edge) % cols, 1)
                 face = jnp.where(lane == spot, moved, face)
-        face_y[turn] = face
-
-        @pl.when(y_to)
-        def _():
-            y_copy(turn).start()
-
-    def arrive(turn):
-        x_from, y_from = gets(turn)
-
-        @pl.when(y_from)
-        def _():
-            y_copy(turn).wait_recv()
-
-        @pl.when(x_from)
-        def _():
-            x_copy(turn).wait_recv()
+        return face
+
+    def start(step):
+        routes = copies(step)
+
+        def go(kind):
+            sends, _, copy = routes[kind]
+
+            @pl.when(sends)
+            def _():
+                copy.start()
+
+        for k, (field, c) in enumerate(((e, 0), (e, 1), (e, 2), (h, 1), (h, 2))):
+            low_out[step, k] = field[c, :, rows - 1, :].astype(jnp.bfloat16)
+        go(0)
+        go(4)
+        for k, c in enumerate((1, 2)):
+            value = e[c, :, 0, :]
+            own[k] = value
+            up_out[step, k] = value.astype(jnp.bfloat16)
+        go(1)
+        pack_out[step, 3] = packed(((e, 1),), cols - 1)
+        go(5)
+        pack_out[step, 1] = packed(((e, 0), (e, 2)), cols - 1)
+        pack_out[step, 2] = packed(((h, 0), (h, 2)), cols - 1)
+        go(3)
+        pack_out[step, 0] = packed(((e, 0), (e, 2)), 0)
+        go(2)
+
+    def arrive(step):
+        for _, gets, copy in copies(step):
+            @pl.when(gets)
+            def _():
+                copy.wait_recv()
+
+    def ghosts(step):
+        c_x = jnp.where(west, COURANT, 0.0)
+        c_y = jnp.where(south, COURANT, 0.0)
+        ex, ey, ez, hy, hz = (low_in[step, k].astype(jnp.float32) for k in range(5))
+        flat_z = lax.broadcasted_iota(jnp.int32, (depth, cols), 0)
+        flat_y = lax.broadcasted_iota(jnp.int32, (depth, cols), 1)
+        corner = pltpu.roll(far_row[step].astype(jnp.float32), cols - 1, 1)
+        ex_z = jnp.where(flat_z == depth - 1, 0.0, pltpu.roll(ex, depth - 1, 0))
+        ex_y = jnp.where(flat_y == cols - 1, corner, pltpu.roll(ex, cols - 1, 1))
+        edge_x[0] = hy - c_x * (ex_z - ex - (own[1] - ez))
+        edge_x[1] = hz - c_x * (own[0] - ey - (ex_y - ex))
+        row = lax.broadcasted_iota(jnp.int32, (rows, cols), 0)
+        e_side, h_side, ey_side = pack_in[step, 1], pack_in[step, 2], pack_in[step, 3]
+        across = pltpu.roll(pack_out[step, 0] - e_side, depth, 1)
+        ey_z = pltpu.roll(ey_side, cols - 1, 1)
+        ey_x = jnp.where(
+            row == rows - 1, pltpu.roll(far_col[step], rows - 1, 0), pltpu.roll(ey_side, rows - 1, 0)
+        )
+        turn_x = across - (ey_z - ey_side)
+        turn_z = pltpu.roll(ey_x - ey_side, depth, 1) - across
+        return h_side - c_y * jnp.where(lane < depth, turn_x, turn_z)
 
     def column(face, first, shift):
         return jnp.stack([pltpu.roll(face, (shift - first - z) % cols, 1) for z in range(CHUNK)])
@@ -163,9 +199,9 @@
             return field[c, base - 1:base - 1 + CHUNK]
         return jnp.concatenate((zero[None], field[c, :CHUNK - 1]), axis=0)
 
-    def magnetic(turn):
-        face = got_y[turn]
-        edge_x[...] = got_x[turn].astype(jnp.float32)
+    def magnetic(step):
+        face = pack_in[step, 0]
+        edge_x[...] = up_in[step].astype(jnp.float32)
         last_row, last_lane = row3 == rows - 1, lane3 == cols - 1
         for base in range(0, depth, CHUNK):
             here = pl.ds(base, CHUNK)
@@ -184,9 +220,7 @@
             h[1, here] = new_y
             h[2, here] = new_z
 
-    def electric(turn):
-        face = got_y[turn]
-        edge_x[...] = got_x[turn].astype(jnp.float32)
+    def electric(face):
         first_row, first_lane = row3 == 0, lane3 == 0
         for base in range(0, depth, CHUNK):
             here = pl.ds(base, CHUNK)
@@ -206,8 +240,6 @@
             e[1, here] = new_y
             e[2, here] = new_z
 
-    loads[0].wait()
-    start(0)
     loads[2].wait()
 
     for base in range(0, depth, CHUNK):
@@ -221,14 +253,14 @@
         drive[base:base + CHUNK] = driven
 
     loads[1].wait()
-    for turn in range(2 * STEPS):
-        if turn:
-            start(turn)
-        arrive(turn)
-        if turn % 2 == 0:
-            magnetic(turn)
-        else:
-            electric(turn)
+    loads[0].wait()
+    start(0)
+    for step in range(STEPS):
+        if step:
+            start(step)
+        arrive(step)
+        magnetic(step)
+        electric(ghosts(step))
 
     def spot(index):
         x_at = pl.multiple_of((index // ny) * rows, rows)
@@ -246,9 +278,9 @@
         return carry
 
     lax.fori_loop(1, nx * ny, push, 0)
-    own = pltpu.make_async_copy(e.at[pl.ds(0, 2), depth - 1], spot(me), n_send.at[0])
-    own.start()
-    own.wait()
+    kept_near = pltpu.make_async_copy(e.at[pl.ds(0, 2), depth - 1], spot(me), n_send.at[0])
+    kept_near.start()
+    kept_near.wait()
 
     def take(step, carry):
         copy = near_copy(
@@ -259,21 +291,16 @@
         return carry
 
     lax.fori_loop(1, nx * ny, take, 0)
-    for turn in range(2 * STEPS):
-        x_to, y_to = sends(turn)
-
-        @pl.when(x_to)
-        def _():
-            x_copy(turn).wait_send()
-
-        @pl.when(y_to)
-        def _():
-            y_copy(turn).wait_send()
+    for step in range(STEPS):
+        for sends, _, copy in copies(step):
+            @pl.when(sends)
+            def _():
+                copy.wait_send()
 
 
 def run_fields(e_field, h_field, material, permittivity, conductivity, nx, ny):
     _, depth, rows, cols = e_field.shape
-    devices, turns = nx * ny, 2 * STEPS
+    devices = nx * ny
     f32, dma = jnp.float32, pltpu.SemaphoreType.DMA
     return pl.pallas_call(
         functools.partial(fields_kernel, nx, ny),
@@ -289,11 +316,16 @@
             pltpu.VMEM((depth, rows, cols), f32),
             pltpu.VMEM((depth, rows, cols), f32),
             pltpu.VMEM((2, depth, cols), f32),
-            pltpu.VMEM((turns, 2, depth, cols), jnp.bfloat16),
-            pltpu.VMEM((turns, rows, cols), f32),
-            pltpu.VMEM((turns, 2, depth, cols), jnp.bfloat16),
-            pltpu.VMEM((turns, rows, cols), f32),
-            dma((3,)), dma((turns,)), dma((turns,)), dma((turns,)), dma((turns,)),
+            pltpu.VMEM((2, depth, cols), f32),
+            pltpu.VMEM((STEPS, 2, depth, cols), jnp.bfloat16),
+            pltpu.VMEM((STEPS, 5, depth, cols), jnp.bfloat16),
+            pltpu.VMEM((STEPS, 4, rows, cols), f32),
+            pltpu.VMEM((STEPS, 2, depth, cols), jnp.bfloat16),
+            pltpu.VMEM((STEPS, 5, depth, cols), jnp.bfloat16),
+            pltpu.VMEM((STEPS, 4, rows, cols), f32),
+            pltpu.VMEM((STEPS, depth, cols), jnp.bfloat16),
+            pltpu.VMEM((STEPS, rows, cols), f32),
+            dma((3,)), dma((STEPS, 6)), dma((STEPS, 6)),
             dma((devices,)), dma((devices,)),
         ],
         compiler_params=pltpu.CompilerParams(

time: 68.6 us -> 61.5 us (0.90)
  Pallas kernels: 61.4 us -> 54.4 us
    pallas_call x1, Pallas kernels: 41 us -> 34.6 us  [run_fields(): pl.pallas_call(functools.partial(fields_kernel, nx, ny), out_shape=(jax.S...]
where the time goes in v5:
time: 61.5 us; the launch traced here: 61.2 us
  Pallas kernels  54.4 us (88%)
  local copies, waits for them, and re-layouts  6.09 us (10%)
  between operations  0.73 us (1%)
    pallas_call x1, Pallas kernels, run_fields(): pl.pallas_call(functools.partial(fields_kernel, nx, ny), out_shape=(jax.S...  34.6 us
    pallas_call x1, Pallas kernels, run_reduce(): pl.pallas_call(functools.partial(reduce_kernel, nx, ny), out_shape=jax.Sh...  11.9 us
    pallas_call x1, Pallas kernels, run_image(): pl.pallas_call(functools.partial(image_kernel, src_shift.shape[0] * devic...  7.93 us
    unnamed x26, local copies, waits for them, and re-layouts  6.09 us

profile of v5, /device:TPU:0, one launch (start us, length us, event | category | flops | bytes accessed | tf_op | source)
XLA Modules:
  0.0 61.2 jit_solution(17619177396653312493)
XLA Ops:
  0.6 0.8 %copy.17.shift = s32[8,2]{1,0:T(8,128)S(1)} copy(s32[8,2]{0,1:T(2,128)} %param.19) | data formatting | bytes 128 | tf_op args[5]
  1.4 0.0 copy-start.1
  1.4 0.0 copy-start.2
  1.4 0.0 copy-start.3
  1.4 0.0 copy-start.5
  1.4 34.6 %fields.1 = (f32[3,64,8,128]{3,2,1,0:T(8,128)}, f32[3,64,8,128]{3,2,1,0:T(8,128)}, f32[2,128,256]{2,1,0:T(8,128)}) custom-call(f32[8]{0:T(128)} %perm.1, f32[8]{0:T(128)} %cond.1, f32[3,64,8,128]{3,2,1,0:T(8,128)} %e_in.1, f32[3,64,8,128]{3,2,1,0:T(8,128)} %h_in.1, s32[64,8,128]{2,1,0:T(8,128)} %mat_in.1), custom_call_target="tpu_custom_call" | custom-call | tf_op jit(solution)/shard_map/fields/pallas_call | solution.py:305
  36.0 0.0 copy-start.8
  36.0 0.0 copy-done.1
  36.0 0.0 copy-done.2
  36.0 0.0 copy-done.3
  36.1 0.0 copy-done.4
  36.1 0.0 copy-done.5
  36.1 0.6 copy-done.8
  36.7 0.9 %copy-done.6 = f32[2,128,256]{2,1,0:T(8,128)S(1)} copy-done((f32[2,128,256]{2,1,0:T(8,128)S(1)}, f32[2,128,256]{2,1,0:T(8,128)}, u32[]{:S(2)}) %copy-start.6) | copy-done | bytes 262168
  37.6 0.8 %copy-done.7 = s32[128,128]{1,0:T(8,128)S(1)} copy-done((s32[128,128]{1,0:T(8,128)S(1)}, s32[128,128]{1,0:T(8,128)}, u32[]{:S(2)}) %copy-start.7) | copy-done | bytes 65560
  38.5 7.9 %sources.1 = bf16[512,256]{1,0:T(8,128)(2,1)S(1)} custom-call(s32[8,2]{1,0:T(8,128)S(1)} %copy.17.shift, f32[8]{0:T(128)S(1)} %copy-done.8, f32[2,128,256]{2,1,0:T(8,128)S(1)} %copy-done.6, f32[256,512]{1,0:T(8,128)S(1)} %copy-done.2, f32[256,256]{1,0:T(8,128)S(1)} %copy-done.5, s32[128,128]{1,0:T(8,128)S(1)} %copy-done.7, bf16[256,512]{1,0:T(8,128)(2,1)S(1)} %copy-done.4, ...), custom_call_target="tpu_custom_call" | custom-call | tf_op jit(solution)/shard_map/sources/pallas_call | solution.py:397
  46.4 0.0 copy-start.10
  46.4 0.0 copy-done
  46.4 11.9 %reduce.1 = f32[16,512]{1,0:T(8,128)S(1)} custom-call(bf16[32,16,256]{2,1,0:T(8,128)(2,1)S(1)} %bitcast.1, f32[256,512]{1,0:T(8,128)S(1)} %copy-done), custom_call_target="tpu_custom_call" | custom-call | tf_op jit(solution)/shard_map/reduce/pallas_call | solution.py:441
  58.3 0.6 %copy.21 = f32[16,512]{1,0:T(8,128)} copy(f32[16,512]{1,0:T(8,128)S(1)} %reduce.1) | data formatting | bytes 65536
  58.9 0.0 copy-done.10
  58.9 0.9 %copy.22 = f32[3,64,8,128]{3,2,1,0:T(8,128)} copy(f32[3,64,8,128]{3,2,1,0:T(8,128)S(1)} %copy-done.10) | data formatting | bytes 1572864
  59.8 0.5 copy-done.9
  60.3 0.9 %copy.23 = f32[3,64,8,128]{3,2,1,0:T(8,128)} copy(f32[3,64,8,128]{3,2,1,0:T(8,128)S(1)} %copy-done.9) | data formatting | bytes 1572864
  (5 shorter events, 0.0 us)
Async XLA Ops:
  1.4 34.6 %copy-start.1 = (f32[512,256]{1,0:T(8,128)S(1)}, f32[512,256]{1,0:T(8,128)}, u32[]{:S(2)}) copy-start(f32[512,256]{1,0:T(8,128)} %constant.16.clone.spread) | copy-start | bytes 1572868
  1.4 34.6 %copy-start.2 = (f32[256,512]{1,0:T(8,128)S(1)}, f32[256,512]{1,0:T(8,128)}, u32[]{:S(2)}) copy-start(f32[256,512]{1,0:T(8,128)} %constant.12.clone.table_y) | copy-start | bytes 1572868
  1.4 34.7 %copy-start.3 = (bf16[512,256]{1,0:T(8,128)(2,1)S(1)}, bf16[512,256]{1,0:T(8,128)(2,1)}, u32[]{:S(2)}) copy-start(bf16[512,256]{1,0:T(8,128)(2,1)} %constant.15.clone.first) | copy-start | bytes 786436
  1.4 34.7 %copy-start.4 = (bf16[256,512]{1,0:T(8,128)(2,1)S(1)}, bf16[256,512]{1,0:T(8,128)(2,1)}, u32[]{:S(2)}) copy-start(bf16[256,512]{1,0:T(8,128)(2,1)} %constant.14.clone.second) | copy-start | bytes 786436
  1.4 34.7 %copy-start.5 = (f32[256,256]{1,0:T(8,128)S(1)}, f32[256,256]{1,0:T(8,128)}, u32[]{:S(2)}) copy-start(f32[256,256]{1,0:T(8,128)} %constant.13.clone.table_x) | copy-start | bytes 786436
  36.0 0.7 %copy-start.8 = (f32[8]{0:T(128)S(1)}, f32[8]{0:T(128)}, u32[]{:S(2)}) copy-start(f32[8]{0:T(128)} %weight.1) | copy-start | bytes 100
  36.7 0.9 %copy-start.6 = (f32[2,128,256]{2,1,0:T(8,128)S(1)}, f32[2,128,256]{2,1,0:T(8,128)}, u32[]{:S(2)}) copy-start(f32[2,128,256]{2,1,0:T(8,128)} %get-tuple-element.6.near) | copy-start | bytes 786436
  37.6 0.8 %copy-start.7 = (s32[128,128]{1,0:T(8,128)S(1)}, s32[128,128]{1,0:T(8,128)}, u32[]{:S(2)}) copy-start(s32[128,128]{1,0:T(8,128)} %mask.1) | copy-start | bytes 196612
  38.5 7.9 %copy-start = (f32[256,512]{1,0:T(8,128)S(1)}, f32[256,512]{1,0:T(8,128)}, u32[]{:S(2)}) copy-start(f32[256,512]{1,0:T(8,128)} %constant.17.clone.spread) | copy-start | bytes 1572868
  46.4 12.5 %copy-start.10 = (f32[3,64,8,128]{3,2,1,0:T(8,128)S(1)}, f32[3,64,8,128]{3,2,1,0:T(8,128)}, u32[]{:S(2)}) copy-start(f32[3,64,8,128]{3,2,1,0:T(8,128)} %get-tuple-element.13) | copy-start | bytes 2359300
  58.9 1.4 %copy-start.9 = (f32[3,64,8,128]{3,2,1,0:T(8,128)S(1)}, f32[3,64,8,128]{3,2,1,0:T(8,128)}, u32[]{:S(2)}) copy-start(f32[3,64,8,128]{3,2,1,0:T(8,128)} %get-tuple-element.14) | copy-start | bytes 2359300

commit v6 on v5

--- a/solution.py
+++ b/solution.py
@@ -139,25 +139,28 @@
             def _():
                 copy.start()
 
-        for k, (field, c) in enumerate(((e, 0), (e, 1), (e, 2), (h, 1), (h, 2))):
-            low_out[step, k] = field[c, :, rows - 1, :].astype(jnp.bfloat16)
-        go(0)
-        go(4)
         for k, c in enumerate((1, 2)):
             value = e[c, :, 0, :]
             own[k] = value
             up_out[step, k] = value.astype(jnp.bfloat16)
         go(1)
+        pack_out[step, 0] = packed(((e, 0), (e, 2)), 0)
+        go(2)
+        for k, (field, c) in enumerate(((e, 0), (e, 1), (e, 2), (h, 1), (h, 2))):
+            low_out[step, k] = field[c, :, rows - 1, :].astype(jnp.bfloat16)
+        go(0)
+        go(4)
         pack_out[step, 3] = packed(((e, 1),), cols - 1)
         go(5)
         pack_out[step, 1] = packed(((e, 0), (e, 2)), cols - 1)
         pack_out[step, 2] = packed(((h, 0), (h, 2)), cols - 1)
         go(3)
-        pack_out[step, 0] = packed(((e, 0), (e, 2)), 0)
-        go(2)
-
-    def arrive(step):
-        for _, gets, copy in copies(step):
+
+    def arrive(step, kinds):
+        routes = copies(step)
+        for kind in kinds:
+            _, gets, copy = routes[kind]
+
             @pl.when(gets)
             def _():
                 copy.wait_recv()
@@ -258,8 +261,9 @@
     for step in range(STEPS):
         if step:
             start(step)
-        arrive(step)
+        arrive(step, (1, 2))
         magnetic(step)
+        arrive(step, (0, 3, 4, 5))
         electric(ghosts(step))
 
     def spot(index):

time: 61.5 us -> 61.3 us (level)
    pallas_call x1, Pallas kernels: 34.6 us -> 33.5 us  [run_fields(): pl.pallas_call(functools.partial(fields_kernel, nx, ny), out_shape=(jax.S...]
    pallas_call x1, Pallas kernels: 11.9 us -> 12.8 us  [run_reduce(): pl.pallas_call(functools.partial(reduce_kernel, nx, ny), out_shape=jax.Sh...]
where the time goes in v6:
time: 61.3 us; the launch traced here: 61 us
  Pallas kernels  54.2 us (88%)
  local copies, waits for them, and re-layouts  6.09 us (10%)
  between operations  0.73 us (1%)
    pallas_call x1, Pallas kernels, run_fields(): pl.pallas_call(functools.partial(fields_kernel, nx, ny), out_shape=(jax.S...  33.5 us
    pallas_call x1, Pallas kernels, run_reduce(): pl.pallas_call(functools.partial(reduce_kernel, nx, ny), out_shape=jax.Sh...  12.8 us
    pallas_call x1, Pallas kernels, run_image(): pl.pallas_call(functools.partial(image_kernel, src_shift.shape[0] * devic...  7.92 us
    unnamed x26, local copies, waits for them, and re-layouts  6.09 us

profile of v6, /device:TPU:0, one launch (start us, length us, event | category | flops | bytes accessed | tf_op | source)
XLA Modules:
  0.0 61.0 jit_solution(12237834136291502513)
XLA Ops:
  0.6 0.8 %copy.17.shift = s32[8,2]{1,0:T(8,128)S(1)} copy(s32[8,2]{0,1:T(2,128)} %param.19) | data formatting | bytes 128 | tf_op args[5]
  1.4 0.0 copy-start.1
  1.4 0.0 copy-start.2
  1.4 0.0 copy-start.3
  1.4 0.0 copy-start.5
  1.4 33.5 %fields.1 = (f32[3,64,8,128]{3,2,1,0:T(8,128)}, f32[3,64,8,128]{3,2,1,0:T(8,128)}, f32[2,128,256]{2,1,0:T(8,128)}) custom-call(f32[8]{0:T(128)} %perm.1, f32[8]{0:T(128)} %cond.1, f32[3,64,8,128]{3,2,1,0:T(8,128)} %e_in.1, f32[3,64,8,128]{3,2,1,0:T(8,128)} %h_in.1, s32[64,8,128]{2,1,0:T(8,128)} %mat_in.1), custom_call_target="tpu_custom_call" | custom-call | tf_op jit(solution)/shard_map/fields/pallas_call | solution.py:309
  34.9 0.0 copy-start.8
  34.9 0.0 copy-done.1
  34.9 0.0 copy-done.2
  34.9 0.0 copy-done.3
  34.9 0.0 copy-done.4
  34.9 0.0 copy-done.5
  34.9 0.6 copy-done.8
  35.5 0.9 %copy-done.6 = f32[2,128,256]{2,1,0:T(8,128)S(1)} copy-done((f32[2,128,256]{2,1,0:T(8,128)S(1)}, f32[2,128,256]{2,1,0:T(8,128)}, u32[]{:S(2)}) %copy-start.6) | copy-done | bytes 262168
  36.5 0.8 %copy-done.7 = s32[128,128]{1,0:T(8,128)S(1)} copy-done((s32[128,128]{1,0:T(8,128)S(1)}, s32[128,128]{1,0:T(8,128)}, u32[]{:S(2)}) %copy-start.7) | copy-done | bytes 65560
  37.3 7.9 %sources.1 = bf16[512,256]{1,0:T(8,128)(2,1)S(1)} custom-call(s32[8,2]{1,0:T(8,128)S(1)} %copy.17.shift, f32[8]{0:T(128)S(1)} %copy-done.8, f32[2,128,256]{2,1,0:T(8,128)S(1)} %copy-done.6, f32[256,512]{1,0:T(8,128)S(1)} %copy-done.2, f32[256,256]{1,0:T(8,128)S(1)} %copy-done.5, s32[128,128]{1,0:T(8,128)S(1)} %copy-done.7, bf16[256,512]{1,0:T(8,128)(2,1)S(1)} %copy-done.4, ...), custom_call_target="tpu_custom_call" | custom-call | tf_op jit(solution)/shard_map/sources/pallas_call | solution.py:401
  45.3 0.0 copy-start.10
  45.3 0.0 copy-done
  45.3 12.8 %reduce.1 = f32[16,512]{1,0:T(8,128)S(1)} custom-call(bf16[32,16,256]{2,1,0:T(8,128)(2,1)S(1)} %bitcast.1, f32[256,512]{1,0:T(8,128)S(1)} %copy-done), custom_call_target="tpu_custom_call" | custom-call | tf_op jit(solution)/shard_map/reduce/pallas_call | solution.py:445
  58.1 0.6 %copy.21 = f32[16,512]{1,0:T(8,128)} copy(f32[16,512]{1,0:T(8,128)S(1)} %reduce.1) | data formatting | bytes 65536
  58.7 0.0 copy-done.10
  58.7 0.9 %copy.22 = f32[3,64,8,128]{3,2,1,0:T(8,128)} copy(f32[3,64,8,128]{3,2,1,0:T(8,128)S(1)} %copy-done.10) | data formatting | bytes 1572864
  59.6 0.5 copy-done.9
  60.2 0.9 %copy.23 = f32[3,64,8,128]{3,2,1,0:T(8,128)} copy(f32[3,64,8,128]{3,2,1,0:T(8,128)S(1)} %copy-done.9) | data formatting | bytes 1572864
  (5 shorter events, 0.0 us)
Async XLA Ops:
  1.4 33.5 %copy-start.1 = (f32[512,256]{1,0:T(8,128)S(1)}, f32[512,256]{1,0:T(8,128)}, u32[]{:S(2)}) copy-start(f32[512,256]{1,0:T(8,128)} %constant.16.clone.spread) | copy-start | bytes 1572868
  1.4 33.5 %copy-start.2 = (f32[256,512]{1,0:T(8,128)S(1)}, f32[256,512]{1,0:T(8,128)}, u32[]{:S(2)}) copy-start(f32[256,512]{1,0:T(8,128)} %constant.12.clone.table_y) | copy-start | bytes 1572868
  1.4 33.5 %copy-start.3 = (bf16[512,256]{1,0:T(8,128)(2,1)S(1)}, bf16[512,256]{1,0:T(8,128)(2,1)}, u32[]{:S(2)}) copy-start(bf16[512,256]{1,0:T(8,128)(2,1)} %constant.15.clone.first) | copy-start | bytes 786436
  1.4 33.5 %copy-start.4 = (bf16[256,512]{1,0:T(8,128)(2,1)S(1)}, bf16[256,512]{1,0:T(8,128)(2,1)}, u32[]{:S(2)}) copy-start(bf16[256,512]{1,0:T(8,128)(2,1)} %constant.14.clone.second) | copy-start | bytes 786436
  1.4 33.5 %copy-start.5 = (f32[256,256]{1,0:T(8,128)S(1)}, f32[256,256]{1,0:T(8,128)}, u32[]{:S(2)}) copy-start(f32[256,256]{1,0:T(8,128)} %constant.13.clone.table_x) | copy-start | bytes 786436
  34.9 0.7 %copy-start.8 = (f32[8]{0:T(128)S(1)}, f32[8]{0:T(128)}, u32[]{:S(2)}) copy-start(f32[8]{0:T(128)} %weight.1) | copy-start | bytes 100
  35.5 0.9 %copy-start.6 = (f32[2,128,256]{2,1,0:T(8,128)S(1)}, f32[2,128,256]{2,1,0:T(8,128)}, u32[]{:S(2)}) copy-start(f32[2,128,256]{2,1,0:T(8,128)} %get-tuple-element.6.near) | copy-start | bytes 786436
  36.5 0.8 %copy-start.7 = (s32[128,128]{1,0:T(8,128)S(1)}, s32[128,128]{1,0:T(8,128)}, u32[]{:S(2)}) copy-start(s32[128,128]{1,0:T(8,128)} %mask.1) | copy-start | bytes 196612
  37.3 7.9 %copy-start = (f32[256,512]{1,0:T(8,128)S(1)}, f32[256,512]{1,0:T(8,128)}, u32[]{:S(2)}) copy-start(f32[256,512]{1,0:T(8,128)} %constant.17.clone.spread) | copy-start | bytes 1572868
  45.3 13.5 %copy-start.10 = (f32[3,64,8,128]{3,2,1,0:T(8,128)S(1)}, f32[3,64,8,128]{3,2,1,0:T(8,128)}, u32[]{:S(2)}) copy-start(f32[3,64,8,128]{3,2,1,0:T(8,128)} %get-tuple-element.13) | copy-start | bytes 2359300
  58.7 1.4 %copy-start.9 = (f32[3,64,8,128]{3,2,1,0:T(8,128)S(1)}, f32[3,64,8,128]{3,2,1,0:T(8,128)}, u32[]{:S(2)}) copy-start(f32[3,64,8,128]{3,2,1,0:T(8,128)} %get-tuple-element.14) | copy-start | bytes 2359300

commit v7 on v6

--- a/solution.py
+++ b/solution.py
@@ -129,6 +129,16 @@
                 face = jnp.where(lane == spot, moved, face)
         return face
 
+    def both_sides(parts):
+        low, high = zero, zero
+        for k, (field, c) in enumerate(parts):
+            for z in range(depth):
+                spot = k * depth + z
+                moved = pltpu.roll(field[c, z], spot, 1) if spot else field[c, z]
+                low = jnp.where(lane == spot, moved, low)
+                high = jnp.where(lane == (spot - 1) % cols, moved, high)
+        return low, pltpu.roll(high, 1, 1)
+
     def start(step):
         routes = copies(step)
 
@@ -144,7 +154,7 @@
             own[k] = value
             up_out[step, k] = value.astype(jnp.bfloat16)
         go(1)
-        pack_out[step, 0] = packed(((e, 0), (e, 2)), 0)
+        pack_out[step, 0], pack_out[step, 1] = both_sides(((e, 0), (e, 2)))
         go(2)
         for k, (field, c) in enumerate(((e, 0), (e, 1), (e, 2), (h, 1), (h, 2))):
             low_out[step, k] = field[c, :, rows - 1, :].astype(jnp.bfloat16)
@@ -152,7 +162,6 @@
         go(4)
         pack_out[step, 3] = packed(((e, 1),), cols - 1)
         go(5)
-        pack_out[step, 1] = packed(((e, 0), (e, 2)), cols - 1)
         pack_out[step, 2] = packed(((h, 0), (h, 2)), cols - 1)
         go(3)
 

time: 61.3 us -> 61.5 us (level)
  no operation moved by 1% of the time
where the time goes in v7:
time: 61.5 us; the launch traced here: 61.2 us
  Pallas kernels  54.3 us (88%)
  local copies, waits for them, and re-layouts  6.09 us (10%)
  between operations  0.73 us (1%)
    pallas_call x1, Pallas kernels, run_fields(): pl.pallas_call(functools.partial(fields_kernel, nx, ny), out_shape=(jax.S...  33.9 us
    pallas_call x1, Pallas kernels, run_reduce(): pl.pallas_call(functools.partial(reduce_kernel, nx, ny), out_shape=jax.Sh...  12.5 us
    pallas_call x1, Pallas kernels, run_image(): pl.pallas_call(functools.partial(image_kernel, src_shift.shape[0] * devic...  7.93 us
    unnamed x26, local copies, waits for them, and re-layouts  6.09 us

profile of v7, /device:TPU:0, one launch (start us, length us, event | category | flops | bytes accessed | tf_op | source)
XLA Modules:
  0.0 61.2 jit_solution(4851147265099907785)
XLA Ops:
  0.6 0.8 %copy.17.shift = s32[8,2]{1,0:T(8,128)S(1)} copy(s32[8,2]{0,1:T(2,128)} %param.19) | data formatting | bytes 128 | tf_op args[5]
  1.4 0.0 copy-start.1
  1.4 0.0 copy-start.3
  1.4 0.0 copy-start.4
  1.4 0.0 copy-start.5
  1.4 33.9 %fields.1 = (f32[3,64,8,128]{3,2,1,0:T(8,128)}, f32[3,64,8,128]{3,2,1,0:T(8,128)}, f32[2,128,256]{2,1,0:T(8,128)}) custom-call(f32[8]{0:T(128)} %perm.1, f32[8]{0:T(128)} %cond.1, f32[3,64,8,128]{3,2,1,0:T(8,128)} %e_in.1, f32[3,64,8,128]{3,2,1,0:T(8,128)} %h_in.1, s32[64,8,128]{2,1,0:T(8,128)} %mat_in.1), custom_call_target="tpu_custom_call" | custom-call | tf_op jit(solution)/shard_map/fields/pallas_call | solution.py:318
  35.3 0.0 copy-start.8
  35.3 0.0 copy-done.1
  35.3 0.0 copy-done.2
  35.3 0.0 copy-done.3
  35.4 0.0 copy-done.4
  35.4 0.0 copy-done.5
  35.4 0.6 copy-done.8
  36.0 0.9 %copy-done.6 = f32[2,128,256]{2,1,0:T(8,128)S(1)} copy-done((f32[2,128,256]{2,1,0:T(8,128)S(1)}, f32[2,128,256]{2,1,0:T(8,128)}, u32[]{:S(2)}) %copy-start.6) | copy-done | bytes 262168
  36.9 0.8 %copy-done.7 = s32[128,128]{1,0:T(8,128)S(1)} copy-done((s32[128,128]{1,0:T(8,128)S(1)}, s32[128,128]{1,0:T(8,128)}, u32[]{:S(2)}) %copy-start.7) | copy-done | bytes 65560
  37.8 7.9 %sources.1 = bf16[512,256]{1,0:T(8,128)(2,1)S(1)} custom-call(s32[8,2]{1,0:T(8,128)S(1)} %copy.17.shift, f32[8]{0:T(128)S(1)} %copy-done.8, f32[2,128,256]{2,1,0:T(8,128)S(1)} %copy-done.6, f32[256,512]{1,0:T(8,128)S(1)} %copy-done.2, f32[256,256]{1,0:T(8,128)S(1)} %copy-done.5, s32[128,128]{1,0:T(8,128)S(1)} %copy-done.7, bf16[256,512]{1,0:T(8,128)(2,1)S(1)} %copy-done.4, ...), custom_call_target="tpu_custom_call" | custom-call | tf_op jit(solution)/shard_map/sources/pallas_call | solution.py:410
  45.7 0.0 copy-start.10
  45.7 0.0 copy-done
  45.7 12.5 %reduce.1 = f32[16,512]{1,0:T(8,128)S(1)} custom-call(bf16[32,16,256]{2,1,0:T(8,128)(2,1)S(1)} %bitcast.1, f32[256,512]{1,0:T(8,128)S(1)} %copy-done), custom_call_target="tpu_custom_call" | custom-call | tf_op jit(solution)/shard_map/reduce/pallas_call | solution.py:454
  58.2 0.6 %copy.21 = f32[16,512]{1,0:T(8,128)} copy(f32[16,512]{1,0:T(8,128)S(1)} %reduce.1) | data formatting | bytes 65536
  58.9 0.0 copy-done.10
  58.9 0.9 %copy.22 = f32[3,64,8,128]{3,2,1,0:T(8,128)} copy(f32[3,64,8,128]{3,2,1,0:T(8,128)S(1)} %copy-done.10) | data formatting | bytes 1572864
  59.8 0.5 copy-done.9
  60.3 0.9 %copy.23 = f32[3,64,8,128]{3,2,1,0:T(8,128)} copy(f32[3,64,8,128]{3,2,1,0:T(8,128)S(1)} %copy-done.9) | data formatting | bytes 1572864
  (5 shorter events, 0.0 us)
Async XLA Ops:
  1.4 33.9 %copy-start.1 = (f32[512,256]{1,0:T(8,128)S(1)}, f32[512,256]{1,0:T(8,128)}, u32[]{:S(2)}) copy-start(f32[512,256]{1,0:T(8,128)} %constant.16.clone.spread) | copy-start | bytes 1572868
  1.4 34.0 %copy-start.2 = (f32[256,512]{1,0:T(8,128)S(1)}, f32[256,512]{1,0:T(8,128)}, u32[]{:S(2)}) copy-start(f32[256,512]{1,0:T(8,128)} %constant.12.clone.table_y) | copy-start | bytes 1572868
  1.4 34.0 %copy-start.3 = (bf16[512,256]{1,0:T(8,128)(2,1)S(1)}, bf16[512,256]{1,0:T(8,128)(2,1)}, u32[]{:S(2)}) copy-start(bf16[512,256]{1,0:T(8,128)(2,1)} %constant.15.clone.first) | copy-start | bytes 786436
  1.4 34.0 %copy-start.4 = (bf16[256,512]{1,0:T(8,128)(2,1)S(1)}, bf16[256,512]{1,0:T(8,128)(2,1)}, u32[]{:S(2)}) copy-start(bf16[256,512]{1,0:T(8,128)(2,1)} %constant.14.clone.second) | copy-start | bytes 786436
  1.4 34.0 %copy-start.5 = (f32[256,256]{1,0:T(8,128)S(1)}, f32[256,256]{1,0:T(8,128)}, u32[]{:S(2)}) copy-start(f32[256,256]{1,0:T(8,128)} %constant.13.clone.table_x) | copy-start | bytes 786436
  35.3 0.7 %copy-start.8 = (f32[8]{0:T(128)S(1)}, f32[8]{0:T(128)}, u32[]{:S(2)}) copy-start(f32[8]{0:T(128)} %weight.1) | copy-start | bytes 100
  36.0 0.9 %copy-start.6 = (f32[2,128,256]{2,1,0:T(8,128)S(1)}, f32[2,128,256]{2,1,0:T(8,128)}, u32[]{:S(2)}) copy-start(f32[2,128,256]{2,1,0:T(8,128)} %get-tuple-element.6.near) | copy-start | bytes 786436
  36.9 0.8 %copy-start.7 = (s32[128,128]{1,0:T(8,128)S(1)}, s32[128,128]{1,0:T(8,128)}, u32[]{:S(2)}) copy-start(s32[128,128]{1,0:T(8,128)} %mask.1) | copy-start | bytes 196612
  37.8 7.9 %copy-start = (f32[256,512]{1,0:T(8,128)S(1)}, f32[256,512]{1,0:T(8,128)}, u32[]{:S(2)}) copy-start(f32[256,512]{1,0:T(8,128)} %constant.17.clone.spread) | copy-start | bytes 1572868
  45.7 13.2 %copy-start.10 = (f32[3,64,8,128]{3,2,1,0:T(8,128)S(1)}, f32[3,64,8,128]{3,2,1,0:T(8,128)}, u32[]{:S(2)}) copy-start(f32[3,64,8,128]{3,2,1,0:T(8,128)} %get-tuple-element.13) | copy-start | bytes 2359300
  58.9 1.4 %copy-start.9 = (f32[3,64,8,128]{3,2,1,0:T(8,128)S(1)}, f32[3,64,8,128]{3,2,1,0:T(8,128)}, u32[]{:S(2)}) copy-start(f32[3,64,8,128]{3,2,1,0:T(8,128)} %get-tuple-element.14) | copy-start | bytes 2359300
